TPU v7x, 32 devices: a whole 2x2x4 slice. The times are simulated.
32 devices in a mesh: expert: 16 (over z, y, x), dp: 2 (over core).
Axes of the slice: x: 2, y: 2, z: 4, core: 2. Of those that a mesh axis runs over, the one named last changes fastest.
Arguments:
- layer_input: bfloat16 [4096, 3584], P(('expert', 'dp')), may hold values from -6 to 6
- out_grad: bfloat16 [4096, 3584], P(('expert', 'dp')), may hold values from -6 to 6
- routes: int32 [4096, 8], P(('expert', 'dp')), may hold values from 0 to 255, as said below
- gate_values: float32 [4096, 8], P(('expert', 'dp')), may hold values from 0.1 to 1
- keep_mask: int32 [4096, 8], P(('expert', 'dp')), may hold values 0 or 1
- gate_weight: bfloat16 [3584, 6144], P('dp', 'expert'), may hold values from -0.09375 to 0.09375
- up_weight: bfloat16 [3584, 6144], P('dp', 'expert'), may hold values from -0.09375 to 0.09375
- down_transposed: bfloat16 [3584, 6144], P('dp', 'expert'), may hold values from -0.15625 to 0.15625
Outputs:
- input_grad: bfloat16 [4096, 3584], P(('expert', 'dp'))
- gate_grad: bfloat16 [3584, 6144], P('dp', 'expert')
- up_grad: bfloat16 [3584, 6144], P('dp', 'expert')
- down_grad: bfloat16 [3584, 6144], P('dp', 'expert')
Inputs may be any that keep to these rules, and one draw needn't show every extreme that they name: `routes`: each token names 8 different experts. Among one device's 128 tokens no expert is named more than 5 times; on every device some expert below 4 is named exactly 5 times, and one expert below 4 is named 5 times on every device.
All inputs are finite; a program needn't handle non-finite values. No bound on the sum of `keep_mask` on one device may be relied on, other than what follows from the above.
Results may differ from a plain program's by a relative error of at most 0.0065.
Values may be sent and summed in bfloat16 or wider, within the bound.
No kernel may reach another device: no remote copies, remote signals or barrier semaphores. Data moves between devices by JAX's collectives and lax.ppermute only.
A program may use at most 128 MiB of HBM per device.

v0:
```python
import jax
import jax.numpy as jnp
from jax import lax
from jax.experimental import pallas as pl
from jax.experimental.pallas import tpu as pltpu
from jax.sharding import PartitionSpec as P

SPLIT = 4
MOST = 5
TOP = 8
SIDES = 2
CORES = 2
GROUPS = 2
FOLDS = 2
FIRST_MIB = 60
CHUNKS = 7

F32 = jnp.float32
BF16 = jnp.bfloat16


def params(mib=16):
    return pltpu.CompilerParams(vmem_limit_bytes=int(mib * 1024 * 1024))


def cost(flops, moved):
    return pl.CostEstimate(flops=int(flops), bytes_accessed=int(moved), transcendentals=0)


def iota(shape, axis):
    return lax.broadcasted_iota(jnp.int32, shape, axis)


def dot(a, b, dims=((1,), (0,))):
    return lax.dot_general(a, b, (dims, ((), ())), preferred_element_type=F32)


def one_hot(wanted, columns):
    return (iota((wanted.shape[0], columns), 1) == wanted).astype(F32).astype(BF16)


def pick_rows(routes, keep, gates, expert, slot, valid):
    rows, tokens = expert.shape[0], routes.shape[1]
    chosen = jnp.zeros((rows, tokens), F32)
    gate = jnp.zeros((rows, tokens), F32)
    for k in range(routes.shape[0]):
        hit = (routes[k : k + 1, :] == expert) & (keep[k : k + 1, :] == 1)
        chosen = jnp.where(hit, 1.0, chosen)
        gate = jnp.where(hit, gates[k : k + 1, :], gate)
    upto = (iota((tokens, tokens), 0) <= iota((tokens, tokens), 1)).astype(F32).astype(BF16)
    rank = dot(chosen.astype(BF16), upto)
    hot = (chosen > 0.5) & (rank == (slot + 1).astype(F32)) & valid
    return hot, gate


def gather_kernel(live, *refs):
    sources, outs, local, sems = refs[:5], refs[5:8], refs[8:13], refs[13]
    copies = [pltpu.make_async_copy(sources[i], local[i], sems.at[i]) for i in range(5)]
    for copy in copies:
        copy.start()
    routes_ref, keep_ref, gates_ref, x_ref, o_ref = local
    place, me = lax.axis_index("expert") // SPLIT, lax.axis_index("dp")
    half = x_ref.shape[1] // CORES
    for copy in copies[:3]:
        copy.wait()
    routes, keep, gates = routes_ref[...], keep_ref[...], gates_ref[...]

    row = iota((live * 8, 1), 0)
    expert, slot = place ^ (row // 8), lax.rem(row, 8)
    hot, _ = pick_rows(routes, keep, gates, expert, slot, slot < MOST)
    outs[2][...] = hot.astype(F32)

    row = iota((live * SIDES * MOST, 1), 0)
    expert = place ^ (row // (SIDES * MOST))
    side, slot = lax.rem(row // MOST, SIDES), lax.rem(row, MOST)
    hot, gate = pick_rows(routes, keep, gates, expert, slot, row >= 0)
    hot_x = (hot & (side == 0)).astype(F32).astype(BF16)
    hot_s = hot & (side == 1)
    scale = jnp.sum(jnp.where(hot_s, gate, 0.0), axis=1, keepdims=True)
    hot_s = hot_s.astype(F32).astype(BF16)
    for copy in copies[3:]:
        copy.wait()
    for q in range(CORES):
        columns = pl.ds(pl.multiple_of((me ^ q) * half, 128), half)
        rows = dot(hot_x, x_ref[:, columns]) + scale * dot(hot_s, o_ref[:, columns])
        outs[q][...] = rows.astype(BF16)


def chunk_kernel(live, mine_ref, other_ref, *outs):
    me = lax.axis_index("dp")
    rows, half = mine_ref.shape
    fold = half // FOLDS
    each = SIDES * MOST
    stacked = jnp.concatenate([mine_ref[...], other_ref[...]], axis=0)
    size = FOLDS * CORES * each
    row = iota((live * size, 1), 0)
    d, part, at = row // size, lax.rem(row // (CORES * each), FOLDS), lax.rem(row, CORES * each)
    wanted = (at // each ^ me) * rows + d * each + lax.rem(at, each)
    total = jnp.zeros((live * size, fold), F32)
    for f in range(FOLDS):
        pick = one_hot(jnp.where(part == f, wanted, -1), CORES * rows)
        total = total + dot(pick, stacked[:, f * fold : (f + 1) * fold])
    total = total.astype(BF16)
    for d in range(live):
        outs[d][...] = total[d * size : (d + 1) * size]


def merge_kernel(*refs):
    chunks, out_ref = refs[:-1], refs[-1]
    size, fold = chunks[0].shape
    stacked = jnp.concatenate([chunk[...] for chunk in chunks], axis=0)
    rows = len(chunks) * CORES * MOST
    out = iota((SIDES * rows, 1), 0)
    side, at = out // rows, lax.rem(out, rows)
    d, replica, slot = at // (CORES * MOST), lax.rem(at // MOST, CORES), lax.rem(at, MOST)
    for f in range(FOLDS):
        wanted = d * size + ((f * CORES + replica) * SIDES + side) * MOST + slot
        picked = dot(one_hot(wanted, len(chunks) * size), stacked)
        out_ref[:, f * fold : (f + 1) * fold] = picked.astype(BF16)


def partial_kernel(*refs):
    blocks, (gate_ref, up_ref, down_ref, out_ref), sided = refs[:SPLIT], refs[SPLIT:-2], refs[-2:]
    each, width = blocks[0].shape[0], gate_ref.shape[1]
    rows = each // SIDES
    stacked = jnp.concatenate([block[...] for block in blocks], axis=0)
    at = iota((SPLIT * rows, 1), 0)
    for side in range(SIDES):
        wanted = at // rows * each + side * rows + lax.rem(at, rows)
        sided[side][...] = dot(one_hot(wanted, SPLIT * each), stacked).astype(BF16)
    out_ref[:, :width] = dot(sided[0][...], gate_ref[...])
    out_ref[:, width : 2 * width] = dot(sided[0][...], up_ref[...])
    out_ref[:, 2 * width :] = dot(sided[1][...], down_ref[...])


def sides_kernel(*refs):
    sums, (gate_ref, up_ref), outs = refs[: 2 * GROUPS], refs[2 * GROUPS : 2 * GROUPS + 2], refs[2 * GROUPS + 2 :]
    parts, sides_ref = outs[:SPLIT], outs[SPLIT]
    width = gate_ref.shape[1]
    rows = parts[0].shape[0]
    total = [sums[i][...] + sums[GROUPS + i][...] for i in range(GROUPS)]
    total = jnp.concatenate(total, axis=0)
    pre_gate, pre_up = total[:, :width], total[:, width : 2 * width]
    hidden_grad = total[:, 2 * width :]
    sigma = jax.nn.sigmoid(pre_gate)
    activated = pre_gate * sigma
    slope = sigma * (1.0 + pre_gate * (1.0 - sigma))
    gate_side = (hidden_grad * pre_up * slope).astype(BF16)
    up_side = (hidden_grad * activated).astype(BF16)
    sides_ref[:, :width] = gate_side
    sides_ref[:, width : 2 * width] = up_side
    sides_ref[:, 2 * width :] = (activated * pre_up).astype(BF16)
    across = ((1,), (1,))
    at = iota((SPLIT * rows, 1), 0)
    k, group, row = at // rows, lax.rem(at, rows) // (rows // GROUPS), lax.rem(at, rows // GROUPS)
    order = one_hot(((GROUPS - 1 - group) * SPLIT + k) * (rows // GROUPS) + row, SPLIT * rows)
    gate_side, up_side = dot(order, gate_side).astype(BF16), dot(order, up_side).astype(BF16)
    part = (dot(gate_side, gate_ref[...], across) + dot(up_side, up_ref[...], across)).astype(BF16)
    for k in range(SPLIT):
        parts[k][...] = part[k * rows : (k + 1) * rows]


def grads_kernel(*refs):
    xs, ss = refs[:GROUPS], refs[GROUPS : 2 * GROUPS]
    sides_ref, outs, token_ref = refs[2 * GROUPS], refs[2 * GROUPS + 1 : -5], refs[-5]
    held, sems = refs[-4:-1], refs[-1]
    half, width = held[0].shape
    block = half // CHUNKS
    first = ((0,), (0,))
    copies = []
    for c in range(CHUNKS):
        part = slice(c * block, (c + 1) * block)
        x = jnp.concatenate([ref[:, part] for ref in xs], axis=0)
        s = jnp.concatenate([ref[:, part] for ref in ss], axis=0)
        for i, rows in enumerate((x, x, s)):
            held[i][part, :] = dot(rows, sides_ref[:, i * width : (i + 1) * width], first).astype(BF16)
            copy = pltpu.make_async_copy(
                held[i].at[pl.ds(c * block, block)], outs[i].at[pl.ds(c * block, block)], sems.at[i, c]
            )
            copy.start()
            copies.append(copy)
    for copy in copies:
        copy.wait()
    token_ref[...] = jnp.zeros(token_ref.shape, F32)


def sum_kernel(live, *refs):
    parts, outs = refs[:SPLIT], refs[SPLIT + 1 :]
    total = parts[0][...].astype(F32)
    for part in parts[1:]:
        total = total + part[...].astype(F32)
    total = total.astype(BF16)
    rows, half = total.shape
    fold = half // FOLDS
    each = CORES * MOST
    size = FOLDS * each
    row = iota((live * size, 1), 0)
    d, part, at = row // size, lax.rem(row // each, FOLDS), lax.rem(row, each)
    moved = jnp.zeros((live * size, fold), F32)
    for f in range(FOLDS):
        pick = one_hot(jnp.where(part == f, d * each + at, -1), rows)
        moved = moved + dot(pick, total[:, f * fold : (f + 1) * fold])
    for d in range(live):
        outs[d][...] = moved[d * size : (d + 1) * size].astype(BF16)


def split_kernel(live, *refs):
    chunks, outs = refs[:live], refs[live:]
    me = lax.axis_index("dp")
    size, fold = chunks[0].shape
    stacked = jnp.concatenate([chunk[...].astype(F32) for chunk in chunks], axis=0).astype(BF16)
    rows = live * 8
    out = iota((CORES * rows, 1), 0)
    q, d, slot = out // rows, lax.rem(out, rows) // 8, lax.rem(out, 8)
    for f in range(FOLDS):
        wanted = d * size + (f * CORES + (q ^ me)) * MOST + slot
        picked = dot(one_hot(jnp.where(slot < MOST, wanted, -1), live * size), stacked).astype(BF16)
        for core in range(CORES):
            outs[core][:, f * fold : (f + 1) * fold] = picked[core * rows : (core + 1) * rows]


def place_kernel(hot_ref, mine_ref, other_ref, out_ref):
    me = lax.axis_index("dp")
    half = mine_ref.shape[1]
    hot = hot_ref[...].astype(BF16)
    for q, ref in enumerate((mine_ref, other_ref)):
        columns = pl.ds(pl.multiple_of((me ^ q) * half, 128), half)
        out_ref[:, columns] = dot(hot, ref[...], ((0,), (0,))).astype(BF16)


def like(shape, dtype):
    return jax.ShapeDtypeStruct(shape, dtype)


def body(
    layer_input, out_grad, routes, gate_values, keep_mask, gate_weight, up_weight, down_transposed
):
    devices = lax.axis_size("expert")
    live = devices // SPLIT
    tokens, model = layer_input.shape
    half, width = gate_weight.shape
    fold = half // FOLDS
    rows = CORES * live * MOST
    total = SPLIT * rows
    vmem, hbm = pl.BlockSpec(memory_space=pltpu.VMEM), pl.BlockSpec(memory_space=pltpu.HBM)

    def call(kernel, name, out_shape, operands, flops=0, moved=0):
        return pl.pallas_call(
            kernel,
            out_shape=out_shape,
            in_specs=[vmem] * len(operands),
            out_specs=jax.tree.map(lambda _: vmem, out_shape),
            compiler_params=params(),
            cost_estimate=cost(flops, moved) if flops else None,
            name=name,
        )(*operands)

    def swap_cores(array):
        return lax.ppermute(array, "dp", [(r, r ^ 1) for r in range(CORES)])

    def along_z(array, d):
        hop = [(i, (i // SPLIT ^ d) * SPLIT + i % SPLIT) for i in range(devices)]
        return lax.ppermute(array, "expert", hop)

    def in_plane(array, k):
        hop = [(i, i // SPLIT * SPLIT + (i % SPLIT ^ k)) for i in range(devices)]
        return lax.ppermute(array, "expert", hop)

    gathered = like((live * SIDES * MOST, half), BF16)
    mine, other, hot = pl.pallas_call(
        lambda *refs: gather_kernel(live, *refs),
        out_shape=[gathered, gathered, like((live * 8, tokens), F32)],
        in_specs=[hbm] * 5,
        out_specs=[vmem] * 3,
        scratch_shapes=[
            pltpu.VMEM((TOP, tokens), jnp.int32),
            pltpu.VMEM((TOP, tokens), jnp.int32),
            pltpu.VMEM((TOP, tokens), F32),
            pltpu.VMEM((tokens, model), BF16),
            pltpu.VMEM((tokens, model), BF16),
            pltpu.SemaphoreType.DMA((5,)),
        ],
        compiler_params=params(FIRST_MIB),
        name="gather_rows",
    )(routes.T, keep_mask.T, gate_values.T, layer_input, out_grad)
    chunks = call(
        lambda *refs: chunk_kernel(live, *refs),
        "chunk_rows",
        [like((FOLDS * CORES * SIDES * MOST, fold), BF16)] * live,
        [mine, swap_cores(other)],
        1e10,
        2e7,
    )
    chunks = [chunks[0]] + [along_z(chunks[d], d) for d in range(1, live)]
    mines, others, xs, ss = [], [], [], []
    rows_in_group, planes = total // GROUPS, live // GROUPS
    for group in reversed(range(GROUPS)):
        rows_here = call(
            merge_kernel,
            "merge_rows",
            like((SIDES * rows // GROUPS, half), BF16),
            chunks[group * planes : (group + 1) * planes],
            1e8,
            1e6,
        )
        by_x, by_y = in_plane(rows_here, 1), in_plane(rows_here, 2)
        across = in_plane(by_y, 1) if group % 2 else in_plane(by_x, 2)
        mine, x, s = call(
            partial_kernel,
            "partial_products",
            [like((rows_in_group, 3 * width), F32)] + [like((rows_in_group, half), BF16)] * SIDES,
            [rows_here, by_x, by_y, across, gate_weight, up_weight, down_transposed],
            6 * rows_in_group * half * width,
            6 * half * width,
        )
        mines.append(mine)
        others.append(swap_cores(mine))
        xs.append(x)
        ss.append(s)
    sided = call(
        sides_kernel,
        "sides_and_parts",
        [like((rows, half), BF16)] * SPLIT + [like((total, 3 * width), BF16)],
        [*mines, *others, gate_weight, up_weight],
        4 * total * half * width,
        4 * half * width,
    )
    parts, sides = sided[:SPLIT], sided[SPLIT]
    parts = [parts[0]] + [in_plane(parts[k], k) for k in range(1, SPLIT)]
    gate_grad, up_grad, down_grad, token = pl.pallas_call(
        grads_kernel,
        out_shape=[like((half, width), BF16)] * 3 + [like((8, 128), F32)],
        in_specs=[vmem] * (2 * GROUPS + 1),
        out_specs=[hbm] * 3 + [vmem],
        scratch_shapes=[pltpu.VMEM((half, width), BF16)] * 3 + [pltpu.SemaphoreType.DMA((3, CHUNKS))],
        compiler_params=params(),
        cost_estimate=cost(6 * total * half * width, 6 * half * width + 4 * total * half),
        name="weight_grads",
    )(*xs, *ss, sides)
    chunks = call(
        lambda *refs: sum_kernel(live, *refs),
        "sum_parts",
        [like((FOLDS * CORES * MOST, fold), BF16)] * live,
        [*parts, token],
    )
    chunks = [chunks[0]] + [along_z(chunks[d], d) for d in range(1, live)]
    back, over = call(
        lambda *refs: split_kernel(live, *refs),
        "split_rows",
        [like((live * 8, half), BF16)] * 2,
        chunks,
    )
    input_grad = call(
        place_kernel, "place_rows", like((tokens, model), BF16), [hot, back, swap_cores(over)]
    )
    return (input_grad, gate_grad, up_grad, down_grad)


def solution(mesh):
    return jax.shard_map(
        body,
        mesh=mesh,
        in_specs=(
            P(("expert", "dp"), None),
            P(("expert", "dp"), None),
            P(("expert", "dp"), None),
            P(("expert", "dp"), None),
            P(("expert", "dp"), None),
            P("dp", "expert"),
            P("dp", "expert"),
            P("dp", "expert"),
        ),
        out_specs=(
            P(("expert", "dp"), None),
            P("dp", "expert"),
            P("dp", "expert"),
            P("dp", "expert"),
        ),
        check_vma=False,
    )
```

profile of v0, /device:TPU:0, one launch (start us, length us, event | category | flops | bytes accessed | tf_op | source)
XLA Modules:
  0.0 56.5 jit_solution(12251374797511467599)
XLA Ops:
  0.6 2.6 %gather_rows.1 = (bf16[40,1792]{1,0:T(8,128)(2,1)}, bf16[40,1792]{1,0:T(8,128)(2,1)}, f32[32,128]{1,0:T(8,128)}) custom-call(s32[8,128]{1,0:T(8,128)} %bitcast.3, s32[8,128]{1,0:T(8,128)} %bitcast.4, f32[8,128]{1,0:T(8,128)} %bitcast.5, bf16[128,3584]{1,0:T(8,128)(2,1)} %refs_3_.1, bf16[128,3584]{1,0:T(8,128)(2,1)} %refs_4_.4), custom_call_target="tpu_custom_call" | custom-call | tf_op jit(solution)/shard_map/gather_rows/pallas_call | solution.py:270
  3.2 0.5 collective-permute-start
  3.8 1.2 %collective-permute-done.refs_1_ = bf16[40,1792]{1,0:T(8,128)(2,1)S(1)} collective-permute-done((bf16[40,1792]{1,0:T(8,128)(2,1)}, bf16[40,1792]{1,0:T(8,128)(2,1)S(1)}, u32[]{:S(2)}, u32[]{:S(2)}) %collective-permute-start) | collective-permute-done | bytes 143392 | tf_op jit(solution)/shard_map/ppermute | solution.py:259
  5.0 0.0 copy-start.4
  5.0 0.9 %copy-done.4 = bf16[40,1792]{1,0:T(8,128)(2,1)S(1)} copy-done((bf16[40,1792]{1,0:T(8,128)(2,1)S(1)}, bf16[40,1792]{1,0:T(8,128)(2,1)}, u32[]{:S(2)}) %copy-start.4) | copy-done | bytes 143384
  5.9 0.0 copy-start
  5.9 0.0 copy-start.1
  5.9 0.0 copy-start.2
  5.9 0.4 chunk_rows.1
  6.3 3.0 %collective-permute-start.6 = (bf16[40,896]{1,0:T(8,128)(2,1)S(1)}, bf16[40,896]{1,0:T(8,128)(2,1)S(1)}, u32[]{:S(2)}, u32[]{:S(2)}) collective-permute-start(bf16[40,896]{1,0:T(8,128)(2,1)S(1)} %get-tuple-element.39), channel_id=1, source_target_pairs={{0,8},{2,10},{4,12},{6,14},{8,0},{10,2},{12,4},{14,6},{16,24},{18,... | collective-permute-start | bytes 215048 | tf_op jit(solution)/shard_map/ppermute | solution.py:263
  9.3 2.6 %collective-permute-start.1 = (bf16[40,896]{1,0:T(8,128)(2,1)S(1)}, bf16[40,896]{1,0:T(8,128)(2,1)S(1)}, u32[]{:S(2)}, u32[]{:S(2)}) collective-permute-start(bf16[40,896]{1,0:T(8,128)(2,1)S(1)} %get-tuple-element.35), channel_id=1, source_target_pairs={{0,16},{2,18},{4,20},{6,22},{8,24},{10,26},{12,28},{14,30},{16,0},... | collective-permute-start | bytes 215048 | tf_op jit(solution)/shard_map/ppermute | solution.py:263
  11.9 0.0 collective-permute-start.2
  11.9 0.0 collective-permute-done.6.refs_1_
  11.9 0.2 merge_rows.3.refs_0_
  12.1 1.8 %collective-permute-start.7 = (bf16[40,1792]{1,0:T(8,128)(2,1)S(1)}, bf16[40,1792]{1,0:T(8,128)(2,1)S(1)}, u32[]{:S(2)}, u32[]{:S(2)}) collective-permute-start(bf16[40,1792]{1,0:T(8,128)(2,1)S(1)} %merge_rows.3.refs_0_), channel_id=1, source_target_pairs={{0,2},{2,0},{4,6},{6,4},{8,10},{10,8},{12,14},{14,12},{16,18},{18,... | collective-permute-start | bytes 430088 | tf_op jit(solution)/shard_map/ppermute | solution.py:267
  13.9 3.3 %collective-permute-done.1.refs_0_ = bf16[40,896]{1,0:T(8,128)(2,1)S(1)} collective-permute-done((bf16[40,896]{1,0:T(8,128)(2,1)S(1)}, bf16[40,896]{1,0:T(8,128)(2,1)S(1)}, u32[]{:S(2)}, u32[]{:S(2)}) %collective-permute-start.1) | collective-permute-done | bytes 71712 | tf_op jit(solution)/shard_map/ppermute | solution.py:263
  17.2 0.9 %collective-permute-done.2.refs_1_ = bf16[40,896]{1,0:T(8,128)(2,1)S(1)} collective-permute-done((bf16[40,896]{1,0:T(8,128)(2,1)S(1)}, bf16[40,896]{1,0:T(8,128)(2,1)S(1)}, u32[]{:S(2)}, u32[]{:S(2)}) %collective-permute-start.2) | collective-permute-done | bytes 71712 | tf_op jit(solution)/shard_map/ppermute | solution.py:263
  18.1 0.2 merge_rows.2.refs_0_
  18.3 1.6 %collective-permute-start.4 = (bf16[40,1792]{1,0:T(8,128)(2,1)S(1)}, bf16[40,1792]{1,0:T(8,128)(2,1)S(1)}, u32[]{:S(2)}, u32[]{:S(2)}) collective-permute-start(bf16[40,1792]{1,0:T(8,128)(2,1)S(1)} %merge_rows.2.refs_0_), channel_id=1, source_target_pairs={{0,4},{2,6},{4,0},{6,2},{8,12},{10,14},{12,8},{14,10},{16,20},{18,... | collective-permute-start | bytes 430088 | tf_op jit(solution)/shard_map/ppermute | solution.py:267
  19.9 0.5 collective-permute-start.8
  20.4 0.0 collective-permute-done.7.refs_1_
  20.4 1.5 %collective-permute-start.9 = (bf16[40,1792]{1,0:T(8,128)(2,1)S(1)}, bf16[40,1792]{1,0:T(8,128)(2,1)S(1)}, u32[]{:S(2)}, u32[]{:S(2)}) collective-permute-start(bf16[40,1792]{1,0:T(8,128)(2,1)S(1)} %collective-permute-done.7.refs_1_), channel_id=1, source_target_pairs={{0,4},{2,6},{4,0},{6,2},{8,12},{10,14},{12,8},{14,10},{16,20},{18,... | collective-permute-start | bytes 430088 | tf_op jit(solution)/shard_map/ppermute | solution.py:267
  21.9 1.5 %collective-permute-start.3 = (bf16[40,1792]{1,0:T(8,128)(2,1)S(1)}, bf16[40,1792]{1,0:T(8,128)(2,1)S(1)}, u32[]{:S(2)}, u32[]{:S(2)}) collective-permute-start(bf16[40,1792]{1,0:T(8,128)(2,1)S(1)} %merge_rows.2.refs_0_), channel_id=1, source_target_pairs={{0,2},{2,0},{4,6},{6,4},{8,10},{10,8},{12,14},{14,12},{16,18},{18,... | collective-permute-start | bytes 430088 | tf_op jit(solution)/shard_map/ppermute | solution.py:267
  23.4 1.7 %collective-permute-done.4.refs_2_ = bf16[40,1792]{1,0:T(8,128)(2,1)S(1)} collective-permute-done((bf16[40,1792]{1,0:T(8,128)(2,1)S(1)}, bf16[40,1792]{1,0:T(8,128)(2,1)S(1)}, u32[]{:S(2)}, u32[]{:S(2)}) %collective-permute-start.4) | collective-permute-done | bytes 143392 | tf_op jit(solution)/shard_map/ppermute | solution.py:267
  25.1 1.5 %collective-permute-start.5 = (bf16[40,1792]{1,0:T(8,128)(2,1)S(1)}, bf16[40,1792]{1,0:T(8,128)(2,1)S(1)}, u32[]{:S(2)}, u32[]{:S(2)}) collective-permute-start(bf16[40,1792]{1,0:T(8,128)(2,1)S(1)} %collective-permute-done.4.refs_2_), channel_id=1, source_target_pairs={{0,2},{2,0},{4,6},{6,4},{8,10},{10,8},{12,14},{14,12},{16,18},{18,... | collective-permute-start | bytes 430088 | tf_op jit(solution)/shard_map/ppermute | solution.py:267
  26.6 0.4 collective-permute-done.8.refs_2_
  27.0 1.5 %collective-permute-done.9.refs_3_ = bf16[40,1792]{1,0:T(8,128)(2,1)S(1)} collective-permute-done((bf16[40,1792]{1,0:T(8,128)(2,1)S(1)}, bf16[40,1792]{1,0:T(8,128)(2,1)S(1)}, u32[]{:S(2)}, u32[]{:S(2)}) %collective-permute-start.9) | collective-permute-done | bytes 143392 | tf_op jit(solution)/shard_map/ppermute | solution.py:267
  28.5 0.0 copy-done
  28.5 0.0 copy-done.1
  28.5 0.0 copy-done.2
  28.5 1.0 %partial_products.3 = (f32[80,1152]{1,0:T(8,128)S(1)}, bf16[80,1792]{1,0:T(8,128)(2,1)S(1)}, bf16[80,1792]{1,0:T(8,128)(2,1)S(1)}) custom-call(bf16[40,1792]{1,0:T(8,128)(2,1)S(1)} %merge_rows.3.refs_0_, bf16[40,1792]{1,0:T(8,128)(2,1)S(1)} %collective-permute-done.7.refs_1_, bf16[40,1792]{1,0:T(8,128)(2,1)S(1)} %collective-permute-done.8.refs_2_, ...), custom_call_target="tpu_custom_call" | custom-call | flops 330301440 | bytes 4128768 | tf_op jit(solution)/shard_map/partial_products/pallas_call | solution.py:248
  29.5 0.1 collective-permute-start.11
  29.6 0.0 collective-permute-done.3.refs_1_
  29.6 0.5 collective-permute-done.5.refs_3_
  30.2 1.0 %partial_products.2 = (f32[80,1152]{1,0:T(8,128)S(1)}, bf16[80,1792]{1,0:T(8,128)(2,1)S(1)}, bf16[80,1792]{1,0:T(8,128)(2,1)S(1)}) custom-call(bf16[40,1792]{1,0:T(8,128)(2,1)S(1)} %merge_rows.2.refs_0_, bf16[40,1792]{1,0:T(8,128)(2,1)S(1)} %collective-permute-done.3.refs_1_, bf16[40,1792]{1,0:T(8,128)(2,1)S(1)} %collective-permute-done.4.refs_2_, ...), custom_call_target="tpu_custom_call" | custom-call | flops 330301440 | bytes 4128768 | tf_op jit(solution)/shard_map/partial_products/pallas_call | solution.py:248
  31.2 0.1 collective-permute-start.10
  31.3 0.0 collective-permute-done.11.refs_3_
  31.3 1.6 %collective-permute-done.10.refs_2_ = f32[80,1152]{1,0:T(8,128)S(1)} collective-permute-done((f32[80,1152]{1,0:T(8,128)S(1)}, f32[80,1152]{1,0:T(8,128)S(1)}, u32[]{:S(2)}, u32[]{:S(2)}) %collective-permute-start.10) | collective-permute-done | bytes 368672 | tf_op jit(solution)/shard_map/ppermute | solution.py:259
  32.9 1.4 %sides_and_parts.1 = (bf16[40,1792]{1,0:T(8,128)(2,1)S(1)}, bf16[40,1792]{1,0:T(8,128)(2,1)S(1)}, bf16[40,1792]{1,0:T(8,128)(2,1)S(1)}, bf16[40,1792]{1,0:T(8,128)(2,1)S(1)}, bf16[160,1152]{1,0:T(8,128)(2,1)S(1)}) custom-call(f32[80,1152]{1,0:T(8,128)S(1)} %get-tuple-element.37.refs_0_, f32[80,1152]{1,0:T(8,128)S(1)} %get-tuple-element.40.refs_1_, ...), custom_call_target="tpu_custom_call" | custom-call | flops 440401920 | bytes 2752512 | tf_op jit(solution)/shard_map/sides_and_parts/pallas_call | solution.py:248
  34.3 1.6 %collective-permute-start.12 = (bf16[40,1792]{1,0:T(8,128)(2,1)S(1)}, bf16[40,1792]{1,0:T(8,128)(2,1)S(1)}, u32[]{:S(2)}, u32[]{:S(2)}) collective-permute-start(bf16[40,1792]{1,0:T(8,128)(2,1)S(1)} %get-tuple-element.42), channel_id=1, source_target_pairs={{0,2},{2,0},{4,6},{6,4},{8,10},{10,8},{12,14},{14,12},{16,18},{18,... | collective-permute-start | bytes 430088 | tf_op jit(solution)/shard_map/ppermute | solution.py:267
  35.9 1.5 %collective-permute-start.13 = (bf16[40,1792]{1,0:T(8,128)(2,1)S(1)}, bf16[40,1792]{1,0:T(8,128)(2,1)S(1)}, u32[]{:S(2)}, u32[]{:S(2)}) collective-permute-start(bf16[40,1792]{1,0:T(8,128)(2,1)S(1)} %get-tuple-element.43), channel_id=1, source_target_pairs={{0,4},{2,6},{4,0},{6,2},{8,12},{10,14},{12,8},{14,10},{16,20},{18,... | collective-permute-start | bytes 430088 | tf_op jit(solution)/shard_map/ppermute | solution.py:267
  37.4 0.5 collective-permute-start.14
  37.9 0.0 copy-start.3
  37.9 2.5 %weight_grads.1 = (bf16[1792,384]{1,0:T(8,128)(2,1)}, bf16[1792,384]{1,0:T(8,128)(2,1)}, bf16[1792,384]{1,0:T(8,128)(2,1)}, f32[8,128]{1,0:T(8,128)S(1)}) custom-call(bf16[80,1792]{1,0:T(8,128)(2,1)S(1)} %get-tuple-element.45.refs_0_, bf16[80,1792]{1,0:T(8,128)(2,1)S(1)} %get-tuple-element.46.refs_1_, bf16[80,1792]{1,0:T(8,128)(2,1)S(1)} %get-tuple-element.47.refs_2_, ...), custom_call_target="tpu_custom_call" | custom-call | flops 660602880 | bytes 5275648 | tf_op jit(solution)/shard_map/weight_grads/pallas_call | solution.py:330
  40.4 0.4 collective-permute-done.12.refs_1_
  40.8 3.7 %collective-permute-done.13.refs_2_ = bf16[40,1792]{1,0:T(8,128)(2,1)S(1)} collective-permute-done((bf16[40,1792]{1,0:T(8,128)(2,1)S(1)}, bf16[40,1792]{1,0:T(8,128)(2,1)S(1)}, u32[]{:S(2)}, u32[]{:S(2)}) %collective-permute-start.13) | collective-permute-done | bytes 143392 | tf_op jit(solution)/shard_map/ppermute | solution.py:267
  44.5 0.0 collective-permute-done.14.refs_3_
  44.5 0.3 sum_parts.1
  44.8 2.3 %collective-permute-start.15 = (bf16[20,896]{1,0:T(8,128)(2,1)S(1)}, bf16[20,896]{1,0:T(8,128)(2,1)S(1)}, u32[]{:S(2)}, u32[]{:S(2)}) collective-permute-start(bf16[20,896]{1,0:T(8,128)(2,1)S(1)} %get-tuple-element.52), channel_id=1, source_target_pairs={{0,8},{2,10},{4,12},{6,14},{8,0},{10,2},{12,4},{14,6},{16,24},{18,... | collective-permute-start | bytes 107528 | tf_op jit(solution)/shard_map/ppermute | solution.py:263
  47.1 0.6 %collective-permute-start.16 = (bf16[20,896]{1,0:T(8,128)(2,1)S(1)}, bf16[20,896]{1,0:T(8,128)(2,1)S(1)}, u32[]{:S(2)}, u32[]{:S(2)}) collective-permute-start(bf16[20,896]{1,0:T(8,128)(2,1)S(1)} %get-tuple-element.53), channel_id=1, source_target_pairs={{0,16},{2,18},{4,20},{6,22},{8,24},{10,26},{12,28},{14,30},{16,0},... | collective-permute-start | bytes 107528 | tf_op jit(solution)/shard_map/ppermute | solution.py:263
  47.7 1.9 %collective-permute-start.17 = (bf16[20,896]{1,0:T(8,128)(2,1)S(1)}, bf16[20,896]{1,0:T(8,128)(2,1)S(1)}, u32[]{:S(2)}, u32[]{:S(2)}) collective-permute-start(bf16[20,896]{1,0:T(8,128)(2,1)S(1)} %get-tuple-element.54), channel_id=1, source_target_pairs={{0,24},{2,26},{4,28},{6,30},{8,16},{10,18},{12,20},{14,22},{16,8},... | collective-permute-start | bytes 107528 | tf_op jit(solution)/shard_map/ppermute | solution.py:263
  49.5 0.0 collective-permute-done.15.refs_1_
  49.5 2.9 %collective-permute-done.16.refs_2_ = bf16[20,896]{1,0:T(8,128)(2,1)S(1)} collective-permute-done((bf16[20,896]{1,0:T(8,128)(2,1)S(1)}, bf16[20,896]{1,0:T(8,128)(2,1)S(1)}, u32[]{:S(2)}, u32[]{:S(2)}) %collective-permute-start.16) | collective-permute-done | bytes 35872 | tf_op jit(solution)/shard_map/ppermute | solution.py:263
  52.4 1.1 %collective-permute-done.17.refs_3_ = bf16[20,896]{1,0:T(8,128)(2,1)S(1)} collective-permute-done((bf16[20,896]{1,0:T(8,128)(2,1)S(1)}, bf16[20,896]{1,0:T(8,128)(2,1)S(1)}, u32[]{:S(2)}, u32[]{:S(2)}) %collective-permute-start.17) | collective-permute-done | bytes 35872 | tf_op jit(solution)/shard_map/ppermute | solution.py:263
  53.5 0.2 split_rows.1
  53.8 0.1 collective-permute-start.18
  53.8 1.3 %collective-permute-done.18.other_ref = bf16[32,1792]{1,0:T(8,128)(2,1)S(1)} collective-permute-done((bf16[32,1792]{1,0:T(8,128)(2,1)S(1)}, bf16[32,1792]{1,0:T(8,128)(2,1)S(1)}, u32[]{:S(2)}, u32[]{:S(2)}) %collective-permute-start.18) | collective-permute-done | bytes 114720 | tf_op jit(solution)/shard_map/ppermute | solution.py:259
  55.2 0.0 copy-done.3
  55.2 1.3 %place_rows.1 = bf16[128,3584]{1,0:T(8,128)(2,1)} custom-call(f32[32,128]{1,0:T(8,128)S(1)} %copy-done.3, bf16[32,1792]{1,0:T(8,128)(2,1)S(1)} %get-tuple-element.55.mine_ref, bf16[32,1792]{1,0:T(8,128)(2,1)S(1)} %collective-permute-done.18.other_ref), custom_call_target="tpu_custom_call" | custom-call | tf_op jit(solution)/shard_map/place_rows/pallas_call | solution.py:248
Async XLA Ops:
  3.2 1.7 %collective-permute-start = (bf16[40,1792]{1,0:T(8,128)(2,1)}, bf16[40,1792]{1,0:T(8,128)(2,1)S(1)}, u32[]{:S(2)}, u32[]{:S(2)}) collective-permute-start(bf16[40,1792]{1,0:T(8,128)(2,1)} %get-tuple-element.34), channel_id=1, source_target_pairs={{0,1},{1,0},{2,3},{3,2},{4,5},{5,4},{6,7},{7,6},{8,9},{9,8},{10,11... | collective-permute-start | bytes 430088 | tf_op jit(solution)/shard_map/ppermute | solution.py:259
  5.0 0.9 %copy-start.4 = (bf16[40,1792]{1,0:T(8,128)(2,1)S(1)}, bf16[40,1792]{1,0:T(8,128)(2,1)}, u32[]{:S(2)}) copy-start(bf16[40,1792]{1,0:T(8,128)(2,1)} %get-tuple-element.33.refs_0_) | copy-start | bytes 430084
  5.9 22.6 %copy-start = (bf16[1792,384]{1,0:T(8,128)(2,1)S(1)}, bf16[1792,384]{1,0:T(8,128)(2,1)}, u32[]{:S(2)}) copy-start(bf16[1792,384]{1,0:T(8,128)(2,1)} %refs_4_.7) | copy-start | bytes 4128772
  5.9 22.6 %copy-start.1 = (bf16[1792,384]{1,0:T(8,128)(2,1)S(1)}, bf16[1792,384]{1,0:T(8,128)(2,1)}, u32[]{:S(2)}) copy-start(bf16[1792,384]{1,0:T(8,128)(2,1)} %refs_5_.5) | copy-start | bytes 4128772
  5.9 22.6 %copy-start.2 = (bf16[1792,384]{1,0:T(8,128)(2,1)S(1)}, bf16[1792,384]{1,0:T(8,128)(2,1)}, u32[]{:S(2)}) copy-start(bf16[1792,384]{1,0:T(8,128)(2,1)} %refs_6_.3) | copy-start | bytes 4128772
  6.3 5.6 %collective-permute-start.6 = (bf16[40,896]{1,0:T(8,128)(2,1)S(1)}, bf16[40,896]{1,0:T(8,128)(2,1)S(1)}, u32[]{:S(2)}, u32[]{:S(2)}) collective-permute-start(bf16[40,896]{1,0:T(8,128)(2,1)S(1)} %get-tuple-element.39), channel_id=1, source_target_pairs={{0,8},{2,10},{4,12},{6,14},{8,0},{10,2},{12,4},{14,6},{16,24},{18,... | collective-permute-start | bytes 215048 | tf_op jit(solution)/shard_map/ppermute | solution.py:263
  9.3 7.9 %collective-permute-start.1 = (bf16[40,896]{1,0:T(8,128)(2,1)S(1)}, bf16[40,896]{1,0:T(8,128)(2,1)S(1)}, u32[]{:S(2)}, u32[]{:S(2)}) collective-permute-start(bf16[40,896]{1,0:T(8,128)(2,1)S(1)} %get-tuple-element.35), channel_id=1, source_target_pairs={{0,16},{2,18},{4,20},{6,22},{8,24},{10,26},{12,28},{14,30},{16,0},... | collective-permute-start | bytes 215048 | tf_op jit(solution)/shard_map/ppermute | solution.py:263
  11.9 6.2 %collective-permute-start.2 = (bf16[40,896]{1,0:T(8,128)(2,1)S(1)}, bf16[40,896]{1,0:T(8,128)(2,1)S(1)}, u32[]{:S(2)}, u32[]{:S(2)}) collective-permute-start(bf16[40,896]{1,0:T(8,128)(2,1)S(1)} %get-tuple-element.36), channel_id=1, source_target_pairs={{0,24},{2,26},{4,28},{6,30},{8,16},{10,18},{12,20},{14,22},{16,8},... | collective-permute-start | bytes 215048 | tf_op jit(solution)/shard_map/ppermute | solution.py:263
  12.1 8.3 %collective-permute-start.7 = (bf16[40,1792]{1,0:T(8,128)(2,1)S(1)}, bf16[40,1792]{1,0:T(8,128)(2,1)S(1)}, u32[]{:S(2)}, u32[]{:S(2)}) collective-permute-start(bf16[40,1792]{1,0:T(8,128)(2,1)S(1)} %merge_rows.3.refs_0_), channel_id=1, source_target_pairs={{0,2},{2,0},{4,6},{6,4},{8,10},{10,8},{12,14},{14,12},{16,18},{18,... | collective-permute-start | bytes 430088 | tf_op jit(solution)/shard_map/ppermute | solution.py:267
  18.3 6.8 %collective-permute-start.4 = (bf16[40,1792]{1,0:T(8,128)(2,1)S(1)}, bf16[40,1792]{1,0:T(8,128)(2,1)S(1)}, u32[]{:S(2)}, u32[]{:S(2)}) collective-permute-start(bf16[40,1792]{1,0:T(8,128)(2,1)S(1)} %merge_rows.2.refs_0_), channel_id=1, source_target_pairs={{0,4},{2,6},{4,0},{6,2},{8,12},{10,14},{12,8},{14,10},{16,20},{18,... | collective-permute-start | bytes 430088 | tf_op jit(solution)/shard_map/ppermute | solution.py:267
  19.9 7.1 %collective-permute-start.8 = (bf16[40,1792]{1,0:T(8,128)(2,1)S(1)}, bf16[40,1792]{1,0:T(8,128)(2,1)S(1)}, u32[]{:S(2)}, u32[]{:S(2)}) collective-permute-start(bf16[40,1792]{1,0:T(8,128)(2,1)S(1)} %merge_rows.3.refs_0_), channel_id=1, source_target_pairs={{0,4},{2,6},{4,0},{6,2},{8,12},{10,14},{12,8},{14,10},{16,20},{18,... | collective-permute-start | bytes 430088 | tf_op jit(solution)/shard_map/ppermute | solution.py:267
  20.4 8.1 %collective-permute-start.9 = (bf16[40,1792]{1,0:T(8,128)(2,1)S(1)}, bf16[40,1792]{1,0:T(8,128)(2,1)S(1)}, u32[]{:S(2)}, u32[]{:S(2)}) collective-permute-start(bf16[40,1792]{1,0:T(8,128)(2,1)S(1)} %collective-permute-done.7.refs_1_), channel_id=1, source_target_pairs={{0,4},{2,6},{4,0},{6,2},{8,12},{10,14},{12,8},{14,10},{16,20},{18,... | collective-permute-start | bytes 430088 | tf_op jit(solution)/shard_map/ppermute | solution.py:267
  21.9 7.7 %collective-permute-start.3 = (bf16[40,1792]{1,0:T(8,128)(2,1)S(1)}, bf16[40,1792]{1,0:T(8,128)(2,1)S(1)}, u32[]{:S(2)}, u32[]{:S(2)}) collective-permute-start(bf16[40,1792]{1,0:T(8,128)(2,1)S(1)} %merge_rows.2.refs_0_), channel_id=1, source_target_pairs={{0,2},{2,0},{4,6},{6,4},{8,10},{10,8},{12,14},{14,12},{16,18},{18,... | collective-permute-start | bytes 430088 | tf_op jit(solution)/shard_map/ppermute | solution.py:267
  25.1 5.1 %collective-permute-start.5 = (bf16[40,1792]{1,0:T(8,128)(2,1)S(1)}, bf16[40,1792]{1,0:T(8,128)(2,1)S(1)}, u32[]{:S(2)}, u32[]{:S(2)}) collective-permute-start(bf16[40,1792]{1,0:T(8,128)(2,1)S(1)} %collective-permute-done.4.refs_2_), channel_id=1, source_target_pairs={{0,2},{2,0},{4,6},{6,4},{8,10},{10,8},{12,14},{14,12},{16,18},{18,... | collective-permute-start | bytes 430088 | tf_op jit(solution)/shard_map/ppermute | solution.py:267
  29.5 1.8 %collective-permute-start.11 = (f32[80,1152]{1,0:T(8,128)S(1)}, f32[80,1152]{1,0:T(8,128)S(1)}, u32[]{:S(2)}, u32[]{:S(2)}) collective-permute-start(f32[80,1152]{1,0:T(8,128)S(1)} %get-tuple-element.40.refs_1_), channel_id=1, source_target_pairs={{0,1},{1,0},{2,3},{3,2},{4,5},{5,4},{6,7},{7,6},{8,9},{9,8},{10,11... | collective-permute-start | bytes 1105928 | tf_op jit(solution)/shard_map/ppermute | solution.py:259
  31.2 1.8 %collective-permute-start.10 = (f32[80,1152]{1,0:T(8,128)S(1)}, f32[80,1152]{1,0:T(8,128)S(1)}, u32[]{:S(2)}, u32[]{:S(2)}) collective-permute-start(f32[80,1152]{1,0:T(8,128)S(1)} %get-tuple-element.37.refs_0_), channel_id=1, source_target_pairs={{0,1},{1,0},{2,3},{3,2},{4,5},{5,4},{6,7},{7,6},{8,9},{9,8},{10,11... | collective-permute-start | bytes 1105928 | tf_op jit(solution)/shard_map/ppermute | solution.py:259
  34.3 6.5 %collective-permute-start.12 = (bf16[40,1792]{1,0:T(8,128)(2,1)S(1)}, bf16[40,1792]{1,0:T(8,128)(2,1)S(1)}, u32[]{:S(2)}, u32[]{:S(2)}) collective-permute-start(bf16[40,1792]{1,0:T(8,128)(2,1)S(1)} %get-tuple-element.42), channel_id=1, source_target_pairs={{0,2},{2,0},{4,6},{6,4},{8,10},{10,8},{12,14},{14,12},{16,18},{18,... | collective-permute-start | bytes 430088 | tf_op jit(solution)/shard_map/ppermute | solution.py:267
  35.9 8.6 %collective-permute-start.13 = (bf16[40,1792]{1,0:T(8,128)(2,1)S(1)}, bf16[40,1792]{1,0:T(8,128)(2,1)S(1)}, u32[]{:S(2)}, u32[]{:S(2)}) collective-permute-start(bf16[40,1792]{1,0:T(8,128)(2,1)S(1)} %get-tuple-element.43), channel_id=1, source_target_pairs={{0,4},{2,6},{4,0},{6,2},{8,12},{10,14},{12,8},{14,10},{16,20},{18,... | collective-permute-start | bytes 430088 | tf_op jit(solution)/shard_map/ppermute | solution.py:267
  37.4 7.1 %collective-permute-start.14 = (bf16[40,1792]{1,0:T(8,128)(2,1)S(1)}, bf16[40,1792]{1,0:T(8,128)(2,1)S(1)}, u32[]{:S(2)}, u32[]{:S(2)}) collective-permute-start(bf16[40,1792]{1,0:T(8,128)(2,1)S(1)} %get-tuple-element.44), channel_id=1, source_target_pairs={{0,6},{2,4},{4,2},{6,0},{8,14},{10,12},{12,10},{14,8},{16,22},{18,... | collective-permute-start | bytes 430088 | tf_op jit(solution)/shard_map/ppermute | solution.py:267
  37.9 17.3 %copy-start.3 = (f32[32,128]{1,0:T(8,128)S(1)}, f32[32,128]{1,0:T(8,128)}, u32[]{:S(2)}) copy-start(f32[32,128]{1,0:T(8,128)} %get-tuple-element.32.hot_ref) | copy-start | bytes 49156
  44.8 4.7 %collective-permute-start.15 = (bf16[20,896]{1,0:T(8,128)(2,1)S(1)}, bf16[20,896]{1,0:T(8,128)(2,1)S(1)}, u32[]{:S(2)}, u32[]{:S(2)}) collective-permute-start(bf16[20,896]{1,0:T(8,128)(2,1)S(1)} %get-tuple-element.52), channel_id=1, source_target_pairs={{0,8},{2,10},{4,12},{6,14},{8,0},{10,2},{12,4},{14,6},{16,24},{18,... | collective-permute-start | bytes 107528 | tf_op jit(solution)/shard_map/ppermute | solution.py:263
  47.1 5.4 %collective-permute-start.16 = (bf16[20,896]{1,0:T(8,128)(2,1)S(1)}, bf16[20,896]{1,0:T(8,128)(2,1)S(1)}, u32[]{:S(2)}, u32[]{:S(2)}) collective-permute-start(bf16[20,896]{1,0:T(8,128)(2,1)S(1)} %get-tuple-element.53), channel_id=1, source_target_pairs={{0,16},{2,18},{4,20},{6,22},{8,24},{10,26},{12,28},{14,30},{16,0},... | collective-permute-start | bytes 107528 | tf_op jit(solution)/shard_map/ppermute | solution.py:263
  47.7 5.9 %collective-permute-start.17 = (bf16[20,896]{1,0:T(8,128)(2,1)S(1)}, bf16[20,896]{1,0:T(8,128)(2,1)S(1)}, u32[]{:S(2)}, u32[]{:S(2)}) collective-permute-start(bf16[20,896]{1,0:T(8,128)(2,1)S(1)} %get-tuple-element.54), channel_id=1, source_target_pairs={{0,24},{2,26},{4,28},{6,30},{8,16},{10,18},{12,20},{14,22},{16,8},... | collective-permute-start | bytes 107528 | tf_op jit(solution)/shard_map/ppermute | solution.py:263
  53.8 1.4 %collective-permute-start.18 = (bf16[32,1792]{1,0:T(8,128)(2,1)S(1)}, bf16[32,1792]{1,0:T(8,128)(2,1)S(1)}, u32[]{:S(2)}, u32[]{:S(2)}) collective-permute-start(bf16[32,1792]{1,0:T(8,128)(2,1)S(1)} %get-tuple-element.56), channel_id=1, source_target_pairs={{0,1},{1,0},{2,3},{3,2},{4,5},{5,4},{6,7},{7,6},{8,9},{9,8},{10,11... | collective-permute-start | bytes 344072 | tf_op jit(solution)/shard_map/ppermute | solution.py:259
where the time goes:
time: 56.7 us; the launch traced here: 56.5 us
  starting transfers between devices  23 us (41%)
  waiting for transfers between devices  20.7 us (37%)
  Pallas kernels  11.2 us (20%)
  local copies, waits for them, and re-layouts  0.92 us (2%)
  between operations  0.76 us (1%)
    ppermute x9, starting transfers between devices, in_plane(): return lax.ppermute(array, 'expert', hop)  11.9 us
    ppermute x6, starting transfers between devices, along_z(): return lax.ppermute(array, 'expert', hop)  10.3 us
    ppermute x6, waiting for transfers between devices, along_z(): return lax.ppermute(array, 'expert', hop)  8.25 us
    ppermute x9, waiting for transfers between devices, in_plane(): return lax.ppermute(array, 'expert', hop)  8.25 us
    pallas_call x9, Pallas kernels, call(): pl.pallas_call(kernel, out_shape=out_shape, in_specs=[vmem] * len(operand...  6.07 us
    ppermute x4, waiting for transfers between devices, swap_cores(): return lax.ppermute(array, 'dp', [(r, r ^ 1) for r in range(CORES)])  4.2 us
    pallas_call x1, Pallas kernels, body(): pl.pallas_call(lambda *refs: gather_kernel(live, *refs), out_shape=[gathe...  2.6 us
    pallas_call x1, Pallas kernels, body(): pl.pallas_call(grads_kernel, out_shape=[like((half, width), BF16)] * 3 +...  2.5 us
  transfers between devices with their start and end apart: 19, of which 13 were waited for; matrix products, arithmetic and copies ran while one was open for 0% of the time, Pallas kernels for 9%

commit v1 on v0

--- a/solution.py
+++ b/solution.py
@@ -51,6 +51,12 @@
     rank = dot(chosen.astype(BF16), upto)
     hot = (chosen > 0.5) & (rank == (slot + 1).astype(F32)) & valid
     return hot, gate
+
+
+def near(k, core):
+    if isinstance(core, int):
+        return 3 - k if core and k in (1, 2) else k
+    return jnp.where((core == 1) & (k > 0) & (k < 3), 3 - k, k)
 
 
 def gather_kernel(live, *refs):
@@ -125,8 +131,9 @@
     rows = each // SIDES
     stacked = jnp.concatenate([block[...] for block in blocks], axis=0)
     at = iota((SPLIT * rows, 1), 0)
+    block = near(at // rows, lax.axis_index("dp"))
     for side in range(SIDES):
-        wanted = at // rows * each + side * rows + lax.rem(at, rows)
+        wanted = block * each + side * rows + lax.rem(at, rows)
         sided[side][...] = dot(one_hot(wanted, SPLIT * each), stacked).astype(BF16)
     out_ref[:, :width] = dot(sided[0][...], gate_ref[...])
     out_ref[:, width : 2 * width] = dot(sided[0][...], up_ref[...])
@@ -152,7 +159,8 @@
     sides_ref[:, 2 * width :] = (activated * pre_up).astype(BF16)
     across = ((1,), (1,))
     at = iota((SPLIT * rows, 1), 0)
-    k, group, row = at // rows, lax.rem(at, rows) // (rows // GROUPS), lax.rem(at, rows // GROUPS)
+    k = near(at // rows, lax.axis_index("dp"))
+    group, row = lax.rem(at, rows) // (rows // GROUPS), lax.rem(at, rows // GROUPS)
     order = one_hot(((GROUPS - 1 - group) * SPLIT + k) * (rows // GROUPS) + row, SPLIT * rows)
     gate_side, up_side = dot(order, gate_side).astype(BF16), dot(order, up_side).astype(BF16)
     part = (dot(gate_side, gate_ref[...], across) + dot(up_side, up_ref[...], across)).astype(BF16)
@@ -263,8 +271,11 @@
         return lax.ppermute(array, "expert", hop)
 
     def in_plane(array, k):
-        hop = [(i, i // SPLIT * SPLIT + (i % SPLIT ^ k)) for i in range(devices)]
-        return lax.ppermute(array, "expert", hop)
+        hop = []
+        for i in range(devices):
+            for r in range(CORES):
+                hop.append((i * CORES + r, (i ^ near(k, r)) * CORES + r))
+        return lax.ppermute(array, ("expert", "dp"), hop)
 
     gathered = like((live * SIDES * MOST, half), BF16)
     mine, other, hot = pl.pallas_call(
@@ -303,13 +314,13 @@
             1e8,
             1e6,
         )
-        by_x, by_y = in_plane(rows_here, 1), in_plane(rows_here, 2)
-        across = in_plane(by_y, 1) if group % 2 else in_plane(by_x, 2)
+        first, second = in_plane(rows_here, 1), in_plane(rows_here, 2)
+        across = in_plane(first, 2)
         mine, x, s = call(
             partial_kernel,
             "partial_products",
             [like((rows_in_group, 3 * width), F32)] + [like((rows_in_group, half), BF16)] * SIDES,
-            [rows_here, by_x, by_y, across, gate_weight, up_weight, down_transposed],
+            [rows_here, first, second, across, gate_weight, up_weight, down_transposed],
             6 * rows_in_group * half * width,
             6 * half * width,
         )

time: 56.7 us -> 56.8 us (level)
  no operation moved by 1% of the time
where the time goes in v1:
time: 56.8 us; the launch traced here: 56.6 us
  starting transfers between devices  22.7 us (40%)
  waiting for transfers between devices  21 us (37%)
  Pallas kernels  11.2 us (20%)
  local copies, waits for them, and re-layouts  0.92 us (2%)
  between operations  0.77 us (1%)
    ppermute x9, starting transfers between devices, in_plane(): return lax.ppermute(array, ('expert', 'dp'), hop)  12 us
    ppermute x6, starting transfers between devices, along_z(): return lax.ppermute(array, 'expert', hop)  10 us
    ppermute x6, waiting for transfers between devices, along_z(): return lax.ppermute(array, 'expert', hop)  8.64 us
    ppermute x9, waiting for transfers between devices, in_plane(): return lax.ppermute(array, ('expert', 'dp'), hop)  8.16 us
    pallas_call x9, Pallas kernels, call(): pl.pallas_call(kernel, out_shape=out_shape, in_specs=[vmem] * len(operand...  6.1 us
    ppermute x4, waiting for transfers between devices, swap_cores(): return lax.ppermute(array, 'dp', [(r, r ^ 1) for r in range(CORES)])  4.19 us
    pallas_call x1, Pallas kernels, body(): pl.pallas_call(lambda *refs: gather_kernel(live, *refs), out_shape=[gathe...  2.6 us
    pallas_call x1, Pallas kernels, body(): pl.pallas_call(grads_kernel, out_shape=[like((half, width), BF16)] * 3 +...  2.5 us
  transfers between devices with their start and end apart: 19, of which 13 were waited for; matrix products, arithmetic and copies ran while one was open for 0% of the time, Pallas kernels for 9%

profile of v1, /device:TPU:0, one launch (start us, length us, event | category | flops | bytes accessed | tf_op | source)
XLA Modules:
  0.0 56.6 jit_solution(927998495486048866)
XLA Ops:
  0.6 2.6 %gather_rows.1 = (bf16[40,1792]{1,0:T(8,128)(2,1)}, bf16[40,1792]{1,0:T(8,128)(2,1)}, f32[32,128]{1,0:T(8,128)}) custom-call(s32[8,128]{1,0:T(8,128)} %bitcast.3, s32[8,128]{1,0:T(8,128)} %bitcast.4, f32[8,128]{1,0:T(8,128)} %bitcast.5, bf16[128,3584]{1,0:T(8,128)(2,1)} %refs_3_.1, bf16[128,3584]{1,0:T(8,128)(2,1)} %refs_4_.4), custom_call_target="tpu_custom_call" | custom-call | tf_op jit(solution)/shard_map/gather_rows/pallas_call | solution.py:281
  3.2 0.5 collective-permute-start
  3.8 1.2 %collective-permute-done.refs_1_ = bf16[40,1792]{1,0:T(8,128)(2,1)S(1)} collective-permute-done((bf16[40,1792]{1,0:T(8,128)(2,1)}, bf16[40,1792]{1,0:T(8,128)(2,1)S(1)}, u32[]{:S(2)}, u32[]{:S(2)}) %collective-permute-start) | collective-permute-done | bytes 143392 | tf_op jit(solution)/shard_map/ppermute | solution.py:267
  5.0 0.0 copy-start.4
  5.0 0.9 %copy-done.4 = bf16[40,1792]{1,0:T(8,128)(2,1)S(1)} copy-done((bf16[40,1792]{1,0:T(8,128)(2,1)S(1)}, bf16[40,1792]{1,0:T(8,128)(2,1)}, u32[]{:S(2)}) %copy-start.4) | copy-done | bytes 143384
  5.9 0.0 copy-start
  5.9 0.0 copy-start.1
  5.9 0.0 copy-start.2
  5.9 0.4 chunk_rows.1
  6.3 3.0 %collective-permute-start.6 = (bf16[40,896]{1,0:T(8,128)(2,1)S(1)}, bf16[40,896]{1,0:T(8,128)(2,1)S(1)}, u32[]{:S(2)}, u32[]{:S(2)}) collective-permute-start(bf16[40,896]{1,0:T(8,128)(2,1)S(1)} %get-tuple-element.39), channel_id=1, source_target_pairs={{0,8},{2,10},{4,12},{6,14},{8,0},{10,2},{12,4},{14,6},{16,24},{18,... | collective-permute-start | bytes 215048 | tf_op jit(solution)/shard_map/ppermute | solution.py:271
  9.3 2.6 %collective-permute-start.1 = (bf16[40,896]{1,0:T(8,128)(2,1)S(1)}, bf16[40,896]{1,0:T(8,128)(2,1)S(1)}, u32[]{:S(2)}, u32[]{:S(2)}) collective-permute-start(bf16[40,896]{1,0:T(8,128)(2,1)S(1)} %get-tuple-element.35), channel_id=1, source_target_pairs={{0,16},{2,18},{4,20},{6,22},{8,24},{10,26},{12,28},{14,30},{16,0},... | collective-permute-start | bytes 215048 | tf_op jit(solution)/shard_map/ppermute | solution.py:271
  11.9 0.0 collective-permute-start.2
  11.9 0.0 collective-permute-done.6.refs_1_
  11.9 0.2 merge_rows.3.refs_0_
  12.1 1.8 %collective-permute-start.7 = (bf16[40,1792]{1,0:T(8,128)(2,1)S(1)}, bf16[40,1792]{1,0:T(8,128)(2,1)S(1)}, u32[]{:S(2)}, u32[]{:S(2)}) collective-permute-start(bf16[40,1792]{1,0:T(8,128)(2,1)S(1)} %merge_rows.3.refs_0_), channel_id=1, source_target_pairs={{0,2},{1,5},{2,0},{3,7},{4,6},{5,1},{6,4},{7,3},{8,10},{9,13},{10,... | collective-permute-start | bytes 430088 | tf_op jit(solution)/shard_map/ppermute | solution.py:278
  13.9 3.3 %collective-permute-done.1.refs_0_ = bf16[40,896]{1,0:T(8,128)(2,1)S(1)} collective-permute-done((bf16[40,896]{1,0:T(8,128)(2,1)S(1)}, bf16[40,896]{1,0:T(8,128)(2,1)S(1)}, u32[]{:S(2)}, u32[]{:S(2)}) %collective-permute-start.1) | collective-permute-done | bytes 71712 | tf_op jit(solution)/shard_map/ppermute | solution.py:271
  17.2 0.9 %collective-permute-done.2.refs_1_ = bf16[40,896]{1,0:T(8,128)(2,1)S(1)} collective-permute-done((bf16[40,896]{1,0:T(8,128)(2,1)S(1)}, bf16[40,896]{1,0:T(8,128)(2,1)S(1)}, u32[]{:S(2)}, u32[]{:S(2)}) %collective-permute-start.2) | collective-permute-done | bytes 71712 | tf_op jit(solution)/shard_map/ppermute | solution.py:271
  18.1 0.2 merge_rows.2.refs_0_
  18.3 1.6 %collective-permute-start.3 = (bf16[40,1792]{1,0:T(8,128)(2,1)S(1)}, bf16[40,1792]{1,0:T(8,128)(2,1)S(1)}, u32[]{:S(2)}, u32[]{:S(2)}) collective-permute-start(bf16[40,1792]{1,0:T(8,128)(2,1)S(1)} %merge_rows.2.refs_0_), channel_id=1, source_target_pairs={{0,2},{1,5},{2,0},{3,7},{4,6},{5,1},{6,4},{7,3},{8,10},{9,13},{10,... | collective-permute-start | bytes 430088 | tf_op jit(solution)/shard_map/ppermute | solution.py:278
  19.9 1.5 %collective-permute-start.8 = (bf16[40,1792]{1,0:T(8,128)(2,1)S(1)}, bf16[40,1792]{1,0:T(8,128)(2,1)S(1)}, u32[]{:S(2)}, u32[]{:S(2)}) collective-permute-start(bf16[40,1792]{1,0:T(8,128)(2,1)S(1)} %merge_rows.3.refs_0_), channel_id=1, source_target_pairs={{0,4},{1,3},{2,6},{3,1},{4,0},{5,7},{6,2},{7,5},{8,12},{9,11},{10,... | collective-permute-start | bytes 430088 | tf_op jit(solution)/shard_map/ppermute | solution.py:278
  21.4 0.0 collective-permute-done.7.refs_1_
  21.4 0.5 collective-permute-start.9
  21.9 1.5 %collective-permute-start.4 = (bf16[40,1792]{1,0:T(8,128)(2,1)S(1)}, bf16[40,1792]{1,0:T(8,128)(2,1)S(1)}, u32[]{:S(2)}, u32[]{:S(2)}) collective-permute-start(bf16[40,1792]{1,0:T(8,128)(2,1)S(1)} %merge_rows.2.refs_0_), channel_id=1, source_target_pairs={{0,4},{1,3},{2,6},{3,1},{4,0},{5,7},{6,2},{7,5},{8,12},{9,11},{10,... | collective-permute-start | bytes 430088 | tf_op jit(solution)/shard_map/ppermute | solution.py:278
  23.4 1.6 %collective-permute-done.3.refs_1_ = bf16[40,1792]{1,0:T(8,128)(2,1)S(1)} collective-permute-done((bf16[40,1792]{1,0:T(8,128)(2,1)S(1)}, bf16[40,1792]{1,0:T(8,128)(2,1)S(1)}, u32[]{:S(2)}, u32[]{:S(2)}) %collective-permute-start.3) | collective-permute-done | bytes 143392 | tf_op jit(solution)/shard_map/ppermute | solution.py:278
  25.1 1.5 %collective-permute-start.5 = (bf16[40,1792]{1,0:T(8,128)(2,1)S(1)}, bf16[40,1792]{1,0:T(8,128)(2,1)S(1)}, u32[]{:S(2)}, u32[]{:S(2)}) collective-permute-start(bf16[40,1792]{1,0:T(8,128)(2,1)S(1)} %collective-permute-done.3.refs_1_), channel_id=1, source_target_pairs={{0,4},{1,3},{2,6},{3,1},{4,0},{5,7},{6,2},{7,5},{8,12},{9,11},{10,... | collective-permute-start | bytes 430088 | tf_op jit(solution)/shard_map/ppermute | solution.py:278
  26.6 0.0 collective-permute-done.8.refs_2_
  26.6 0.0 collective-permute-done.9.refs_3_
  26.6 0.0 copy-done
  26.6 0.0 copy-done.1
  26.6 0.0 copy-done.2
  26.6 1.0 %partial_products.3 = (f32[80,1152]{1,0:T(8,128)S(1)}, bf16[80,1792]{1,0:T(8,128)(2,1)S(1)}, bf16[80,1792]{1,0:T(8,128)(2,1)S(1)}) custom-call(bf16[40,1792]{1,0:T(8,128)(2,1)S(1)} %merge_rows.3.refs_0_, bf16[40,1792]{1,0:T(8,128)(2,1)S(1)} %collective-permute-done.7.refs_1_, bf16[40,1792]{1,0:T(8,128)(2,1)S(1)} %collective-permute-done.8.refs_2_, ...), custom_call_target="tpu_custom_call" | custom-call | flops 330301440 | bytes 4128768 | tf_op jit(solution)/shard_map/partial_products/pallas_call | solution.py:256
  27.6 0.1 collective-permute-start.11
  27.7 0.3 collective-permute-done.4.refs_2_
  28.0 2.1 %collective-permute-done.5.refs_3_ = bf16[40,1792]{1,0:T(8,128)(2,1)S(1)} collective-permute-done((bf16[40,1792]{1,0:T(8,128)(2,1)S(1)}, bf16[40,1792]{1,0:T(8,128)(2,1)S(1)}, u32[]{:S(2)}, u32[]{:S(2)}) %collective-permute-start.5) | collective-permute-done | bytes 143392 | tf_op jit(solution)/shard_map/ppermute | solution.py:278
  30.2 1.0 %partial_products.2 = (f32[80,1152]{1,0:T(8,128)S(1)}, bf16[80,1792]{1,0:T(8,128)(2,1)S(1)}, bf16[80,1792]{1,0:T(8,128)(2,1)S(1)}) custom-call(bf16[40,1792]{1,0:T(8,128)(2,1)S(1)} %merge_rows.2.refs_0_, bf16[40,1792]{1,0:T(8,128)(2,1)S(1)} %collective-permute-done.3.refs_1_, bf16[40,1792]{1,0:T(8,128)(2,1)S(1)} %collective-permute-done.4.refs_2_, ...), custom_call_target="tpu_custom_call" | custom-call | flops 330301440 | bytes 4128768 | tf_op jit(solution)/shard_map/partial_products/pallas_call | solution.py:256
  31.2 0.1 collective-permute-start.10
  31.3 0.0 collective-permute-done.11.refs_3_
  31.3 1.7 %collective-permute-done.10.refs_2_ = f32[80,1152]{1,0:T(8,128)S(1)} collective-permute-done((f32[80,1152]{1,0:T(8,128)S(1)}, f32[80,1152]{1,0:T(8,128)S(1)}, u32[]{:S(2)}, u32[]{:S(2)}) %collective-permute-start.10) | collective-permute-done | bytes 368672 | tf_op jit(solution)/shard_map/ppermute | solution.py:267
  32.9 1.4 %sides_and_parts.1 = (bf16[40,1792]{1,0:T(8,128)(2,1)S(1)}, bf16[40,1792]{1,0:T(8,128)(2,1)S(1)}, bf16[40,1792]{1,0:T(8,128)(2,1)S(1)}, bf16[40,1792]{1,0:T(8,128)(2,1)S(1)}, bf16[160,1152]{1,0:T(8,128)(2,1)S(1)}) custom-call(f32[80,1152]{1,0:T(8,128)S(1)} %get-tuple-element.37.refs_0_, f32[80,1152]{1,0:T(8,128)S(1)} %get-tuple-element.40.refs_1_, ...), custom_call_target="tpu_custom_call" | custom-call | flops 440401920 | bytes 2752512 | tf_op jit(solution)/shard_map/sides_and_parts/pallas_call | solution.py:256
  34.4 1.6 %collective-permute-start.12 = (bf16[40,1792]{1,0:T(8,128)(2,1)S(1)}, bf16[40,1792]{1,0:T(8,128)(2,1)S(1)}, u32[]{:S(2)}, u32[]{:S(2)}) collective-permute-start(bf16[40,1792]{1,0:T(8,128)(2,1)S(1)} %get-tuple-element.42), channel_id=1, source_target_pairs={{0,2},{1,5},{2,0},{3,7},{4,6},{5,1},{6,4},{7,3},{8,10},{9,13},{10,... | collective-permute-start | bytes 430088 | tf_op jit(solution)/shard_map/ppermute | solution.py:278
  35.9 1.5 %collective-permute-start.13 = (bf16[40,1792]{1,0:T(8,128)(2,1)S(1)}, bf16[40,1792]{1,0:T(8,128)(2,1)S(1)}, u32[]{:S(2)}, u32[]{:S(2)}) collective-permute-start(bf16[40,1792]{1,0:T(8,128)(2,1)S(1)} %get-tuple-element.43), channel_id=1, source_target_pairs={{0,4},{1,3},{2,6},{3,1},{4,0},{5,7},{6,2},{7,5},{8,12},{9,11},{10,... | collective-permute-start | bytes 430088 | tf_op jit(solution)/shard_map/ppermute | solution.py:278
  37.5 0.5 collective-permute-start.14
  37.9 0.0 copy-start.3
  37.9 2.5 %weight_grads.1 = (bf16[1792,384]{1,0:T(8,128)(2,1)}, bf16[1792,384]{1,0:T(8,128)(2,1)}, bf16[1792,384]{1,0:T(8,128)(2,1)}, f32[8,128]{1,0:T(8,128)S(1)}) custom-call(bf16[80,1792]{1,0:T(8,128)(2,1)S(1)} %get-tuple-element.45.refs_0_, bf16[80,1792]{1,0:T(8,128)(2,1)S(1)} %get-tuple-element.46.refs_1_, bf16[80,1792]{1,0:T(8,128)(2,1)S(1)} %get-tuple-element.47.refs_2_, ...), custom_call_target="tpu_custom_call" | custom-call | flops 660602880 | bytes 5275648 | tf_op jit(solution)/shard_map/weight_grads/pallas_call | solution.py:341
  40.4 0.3 collective-permute-done.12.refs_1_
  40.7 0.4 collective-permute-done.13.refs_2_
  41.2 3.3 %collective-permute-done.14.refs_3_ = bf16[40,1792]{1,0:T(8,128)(2,1)S(1)} collective-permute-done((bf16[40,1792]{1,0:T(8,128)(2,1)S(1)}, bf16[40,1792]{1,0:T(8,128)(2,1)S(1)}, u32[]{:S(2)}, u32[]{:S(2)}) %collective-permute-start.14) | collective-permute-done | bytes 143392 | tf_op jit(solution)/shard_map/ppermute | solution.py:278
  44.5 0.3 sum_parts.1
  44.8 1.3 %collective-permute-start.15 = (bf16[20,896]{1,0:T(8,128)(2,1)S(1)}, bf16[20,896]{1,0:T(8,128)(2,1)S(1)}, u32[]{:S(2)}, u32[]{:S(2)}) collective-permute-start(bf16[20,896]{1,0:T(8,128)(2,1)S(1)} %get-tuple-element.52), channel_id=1, source_target_pairs={{0,8},{2,10},{4,12},{6,14},{8,0},{10,2},{12,4},{14,6},{16,24},{18,... | collective-permute-start | bytes 107528 | tf_op jit(solution)/shard_map/ppermute | solution.py:271
  46.1 1.7 %collective-permute-start.16 = (bf16[20,896]{1,0:T(8,128)(2,1)S(1)}, bf16[20,896]{1,0:T(8,128)(2,1)S(1)}, u32[]{:S(2)}, u32[]{:S(2)}) collective-permute-start(bf16[20,896]{1,0:T(8,128)(2,1)S(1)} %get-tuple-element.53), channel_id=1, source_target_pairs={{0,16},{2,18},{4,20},{6,22},{8,24},{10,26},{12,28},{14,30},{16,0},... | collective-permute-start | bytes 107528 | tf_op jit(solution)/shard_map/ppermute | solution.py:271
  47.8 1.4 %collective-permute-start.17 = (bf16[20,896]{1,0:T(8,128)(2,1)S(1)}, bf16[20,896]{1,0:T(8,128)(2,1)S(1)}, u32[]{:S(2)}, u32[]{:S(2)}) collective-permute-start(bf16[20,896]{1,0:T(8,128)(2,1)S(1)} %get-tuple-element.54), channel_id=1, source_target_pairs={{0,24},{2,26},{4,28},{6,30},{8,16},{10,18},{12,20},{14,22},{16,8},... | collective-permute-start | bytes 107528 | tf_op jit(solution)/shard_map/ppermute | solution.py:271
  49.2 0.0 collective-permute-done.15.refs_1_
  49.2 2.7 %collective-permute-done.16.refs_2_ = bf16[20,896]{1,0:T(8,128)(2,1)S(1)} collective-permute-done((bf16[20,896]{1,0:T(8,128)(2,1)S(1)}, bf16[20,896]{1,0:T(8,128)(2,1)S(1)}, u32[]{:S(2)}, u32[]{:S(2)}) %collective-permute-start.16) | collective-permute-done | bytes 35872 | tf_op jit(solution)/shard_map/ppermute | solution.py:271
  51.9 1.7 %collective-permute-done.17.refs_3_ = bf16[20,896]{1,0:T(8,128)(2,1)S(1)} collective-permute-done((bf16[20,896]{1,0:T(8,128)(2,1)S(1)}, bf16[20,896]{1,0:T(8,128)(2,1)S(1)}, u32[]{:S(2)}, u32[]{:S(2)}) %collective-permute-start.17) | collective-permute-done | bytes 35872 | tf_op jit(solution)/shard_map/ppermute | solution.py:271
  53.6 0.2 split_rows.1
  53.9 0.1 collective-permute-start.18
  53.9 1.3 %collective-permute-done.18.other_ref = bf16[32,1792]{1,0:T(8,128)(2,1)S(1)} collective-permute-done((bf16[32,1792]{1,0:T(8,128)(2,1)S(1)}, bf16[32,1792]{1,0:T(8,128)(2,1)S(1)}, u32[]{:S(2)}, u32[]{:S(2)}) %collective-permute-start.18) | collective-permute-done | bytes 114720 | tf_op jit(solution)/shard_map/ppermute | solution.py:267
  55.3 0.0 copy-done.3
  55.3 1.3 %place_rows.1 = bf16[128,3584]{1,0:T(8,128)(2,1)} custom-call(f32[32,128]{1,0:T(8,128)S(1)} %copy-done.3, bf16[32,1792]{1,0:T(8,128)(2,1)S(1)} %get-tuple-element.55.mine_ref, bf16[32,1792]{1,0:T(8,128)(2,1)S(1)} %collective-permute-done.18.other_ref), custom_call_target="tpu_custom_call" | custom-call | tf_op jit(solution)/shard_map/place_rows/pallas_call | solution.py:256
Async XLA Ops:
  3.2 1.7 %collective-permute-start = (bf16[40,1792]{1,0:T(8,128)(2,1)}, bf16[40,1792]{1,0:T(8,128)(2,1)S(1)}, u32[]{:S(2)}, u32[]{:S(2)}) collective-permute-start(bf16[40,1792]{1,0:T(8,128)(2,1)} %get-tuple-element.34), channel_id=1, source_target_pairs={{0,1},{1,0},{2,3},{3,2},{4,5},{5,4},{6,7},{7,6},{8,9},{9,8},{10,11... | collective-permute-start | bytes 430088 | tf_op jit(solution)/shard_map/ppermute | solution.py:267
  5.0 0.9 %copy-start.4 = (bf16[40,1792]{1,0:T(8,128)(2,1)S(1)}, bf16[40,1792]{1,0:T(8,128)(2,1)}, u32[]{:S(2)}) copy-start(bf16[40,1792]{1,0:T(8,128)(2,1)} %get-tuple-element.33.refs_0_) | copy-start | bytes 430084
  5.9 20.7 %copy-start = (bf16[1792,384]{1,0:T(8,128)(2,1)S(1)}, bf16[1792,384]{1,0:T(8,128)(2,1)}, u32[]{:S(2)}) copy-start(bf16[1792,384]{1,0:T(8,128)(2,1)} %refs_4_.7) | copy-start | bytes 4128772
  5.9 20.7 %copy-start.1 = (bf16[1792,384]{1,0:T(8,128)(2,1)S(1)}, bf16[1792,384]{1,0:T(8,128)(2,1)}, u32[]{:S(2)}) copy-start(bf16[1792,384]{1,0:T(8,128)(2,1)} %refs_5_.5) | copy-start | bytes 4128772
  5.9 20.7 %copy-start.2 = (bf16[1792,384]{1,0:T(8,128)(2,1)S(1)}, bf16[1792,384]{1,0:T(8,128)(2,1)}, u32[]{:S(2)}) copy-start(bf16[1792,384]{1,0:T(8,128)(2,1)} %refs_6_.3) | copy-start | bytes 4128772
  6.3 5.6 %collective-permute-start.6 = (bf16[40,896]{1,0:T(8,128)(2,1)S(1)}, bf16[40,896]{1,0:T(8,128)(2,1)S(1)}, u32[]{:S(2)}, u32[]{:S(2)}) collective-permute-start(bf16[40,896]{1,0:T(8,128)(2,1)S(1)} %get-tuple-element.39), channel_id=1, source_target_pairs={{0,8},{2,10},{4,12},{6,14},{8,0},{10,2},{12,4},{14,6},{16,24},{18,... | collective-permute-start | bytes 215048 | tf_op jit(solution)/shard_map/ppermute | solution.py:271
  9.3 7.9 %collective-permute-start.1 = (bf16[40,896]{1,0:T(8,128)(2,1)S(1)}, bf16[40,896]{1,0:T(8,128)(2,1)S(1)}, u32[]{:S(2)}, u32[]{:S(2)}) collective-permute-start(bf16[40,896]{1,0:T(8,128)(2,1)S(1)} %get-tuple-element.35), channel_id=1, source_target_pairs={{0,16},{2,18},{4,20},{6,22},{8,24},{10,26},{12,28},{14,30},{16,0},... | collective-permute-start | bytes 215048 | tf_op jit(solution)/shard_map/ppermute | solution.py:271
  11.9 6.2 %collective-permute-start.2 = (bf16[40,896]{1,0:T(8,128)(2,1)S(1)}, bf16[40,896]{1,0:T(8,128)(2,1)S(1)}, u32[]{:S(2)}, u32[]{:S(2)}) collective-permute-start(bf16[40,896]{1,0:T(8,128)(2,1)S(1)} %get-tuple-element.36), channel_id=1, source_target_pairs={{0,24},{2,26},{4,28},{6,30},{8,16},{10,18},{12,20},{14,22},{16,8},... | collective-permute-start | bytes 215048 | tf_op jit(solution)/shard_map/ppermute | solution.py:271
  12.1 9.3 %collective-permute-start.7 = (bf16[40,1792]{1,0:T(8,128)(2,1)S(1)}, bf16[40,1792]{1,0:T(8,128)(2,1)S(1)}, u32[]{:S(2)}, u32[]{:S(2)}) collective-permute-start(bf16[40,1792]{1,0:T(8,128)(2,1)S(1)} %merge_rows.3.refs_0_), channel_id=1, source_target_pairs={{0,2},{1,5},{2,0},{3,7},{4,6},{5,1},{6,4},{7,3},{8,10},{9,13},{10,... | collective-permute-start | bytes 430088 | tf_op jit(solution)/shard_map/ppermute | solution.py:278
  18.3 6.8 %collective-permute-start.3 = (bf16[40,1792]{1,0:T(8,128)(2,1)S(1)}, bf16[40,1792]{1,0:T(8,128)(2,1)S(1)}, u32[]{:S(2)}, u32[]{:S(2)}) collective-permute-start(bf16[40,1792]{1,0:T(8,128)(2,1)S(1)} %merge_rows.2.refs_0_), channel_id=1, source_target_pairs={{0,2},{1,5},{2,0},{3,7},{4,6},{5,1},{6,4},{7,3},{8,10},{9,13},{10,... | collective-permute-start | bytes 430088 | tf_op jit(solution)/shard_map/ppermute | solution.py:278
  19.9 6.7 %collective-permute-start.8 = (bf16[40,1792]{1,0:T(8,128)(2,1)S(1)}, bf16[40,1792]{1,0:T(8,128)(2,1)S(1)}, u32[]{:S(2)}, u32[]{:S(2)}) collective-permute-start(bf16[40,1792]{1,0:T(8,128)(2,1)S(1)} %merge_rows.3.refs_0_), channel_id=1, source_target_pairs={{0,4},{1,3},{2,6},{3,1},{4,0},{5,7},{6,2},{7,5},{8,12},{9,11},{10,... | collective-permute-start | bytes 430088 | tf_op jit(solution)/shard_map/ppermute | solution.py:278
  21.4 5.2 %collective-permute-start.9 = (bf16[40,1792]{1,0:T(8,128)(2,1)S(1)}, bf16[40,1792]{1,0:T(8,128)(2,1)S(1)}, u32[]{:S(2)}, u32[]{:S(2)}) collective-permute-start(bf16[40,1792]{1,0:T(8,128)(2,1)S(1)} %collective-permute-done.7.refs_1_), channel_id=1, source_target_pairs={{0,4},{1,3},{2,6},{3,1},{4,0},{5,7},{6,2},{7,5},{8,12},{9,11},{10,... | collective-permute-start | bytes 430088 | tf_op jit(solution)/shard_map/ppermute | solution.py:278
  21.9 6.1 %collective-permute-start.4 = (bf16[40,1792]{1,0:T(8,128)(2,1)S(1)}, bf16[40,1792]{1,0:T(8,128)(2,1)S(1)}, u32[]{:S(2)}, u32[]{:S(2)}) collective-permute-start(bf16[40,1792]{1,0:T(8,128)(2,1)S(1)} %merge_rows.2.refs_0_), channel_id=1, source_target_pairs={{0,4},{1,3},{2,6},{3,1},{4,0},{5,7},{6,2},{7,5},{8,12},{9,11},{10,... | collective-permute-start | bytes 430088 | tf_op jit(solution)/shard_map/ppermute | solution.py:278
  25.1 5.1 %collective-permute-start.5 = (bf16[40,1792]{1,0:T(8,128)(2,1)S(1)}, bf16[40,1792]{1,0:T(8,128)(2,1)S(1)}, u32[]{:S(2)}, u32[]{:S(2)}) collective-permute-start(bf16[40,1792]{1,0:T(8,128)(2,1)S(1)} %collective-permute-done.3.refs_1_), channel_id=1, source_target_pairs={{0,4},{1,3},{2,6},{3,1},{4,0},{5,7},{6,2},{7,5},{8,12},{9,11},{10,... | collective-permute-start | bytes 430088 | tf_op jit(solution)/shard_map/ppermute | solution.py:278
  27.6 3.6 %collective-permute-start.11 = (f32[80,1152]{1,0:T(8,128)S(1)}, f32[80,1152]{1,0:T(8,128)S(1)}, u32[]{:S(2)}, u32[]{:S(2)}) collective-permute-start(f32[80,1152]{1,0:T(8,128)S(1)} %get-tuple-element.40.refs_1_), channel_id=1, source_target_pairs={{0,1},{1,0},{2,3},{3,2},{4,5},{5,4},{6,7},{7,6},{8,9},{9,8},{10,11... | collective-permute-start | bytes 1105928 | tf_op jit(solution)/shard_map/ppermute | solution.py:267
  31.2 1.8 %collective-permute-start.10 = (f32[80,1152]{1,0:T(8,128)S(1)}, f32[80,1152]{1,0:T(8,128)S(1)}, u32[]{:S(2)}, u32[]{:S(2)}) collective-permute-start(f32[80,1152]{1,0:T(8,128)S(1)} %get-tuple-element.37.refs_0_), channel_id=1, source_target_pairs={{0,1},{1,0},{2,3},{3,2},{4,5},{5,4},{6,7},{7,6},{8,9},{9,8},{10,11... | collective-permute-start | bytes 1105928 | tf_op jit(solution)/shard_map/ppermute | solution.py:267
  34.4 6.4 %collective-permute-start.12 = (bf16[40,1792]{1,0:T(8,128)(2,1)S(1)}, bf16[40,1792]{1,0:T(8,128)(2,1)S(1)}, u32[]{:S(2)}, u32[]{:S(2)}) collective-permute-start(bf16[40,1792]{1,0:T(8,128)(2,1)S(1)} %get-tuple-element.42), channel_id=1, source_target_pairs={{0,2},{1,5},{2,0},{3,7},{4,6},{5,1},{6,4},{7,3},{8,10},{9,13},{10,... | collective-permute-start | bytes 430088 | tf_op jit(solution)/shard_map/ppermute | solution.py:278
  35.9 5.3 %collective-permute-start.13 = (bf16[40,1792]{1,0:T(8,128)(2,1)S(1)}, bf16[40,1792]{1,0:T(8,128)(2,1)S(1)}, u32[]{:S(2)}, u32[]{:S(2)}) collective-permute-start(bf16[40,1792]{1,0:T(8,128)(2,1)S(1)} %get-tuple-element.43), channel_id=1, source_target_pairs={{0,4},{1,3},{2,6},{3,1},{4,0},{5,7},{6,2},{7,5},{8,12},{9,11},{10,... | collective-permute-start | bytes 430088 | tf_op jit(solution)/shard_map/ppermute | solution.py:278
  37.5 7.0 %collective-permute-start.14 = (bf16[40,1792]{1,0:T(8,128)(2,1)S(1)}, bf16[40,1792]{1,0:T(8,128)(2,1)S(1)}, u32[]{:S(2)}, u32[]{:S(2)}) collective-permute-start(bf16[40,1792]{1,0:T(8,128)(2,1)S(1)} %get-tuple-element.44), channel_id=1, source_target_pairs={{0,6},{1,7},{2,4},{3,5},{4,2},{5,3},{6,0},{7,1},{8,14},{9,15},{10,... | collective-permute-start | bytes 430088 | tf_op jit(solution)/shard_map/ppermute | solution.py:278
  37.9 17.3 %copy-start.3 = (f32[32,128]{1,0:T(8,128)S(1)}, f32[32,128]{1,0:T(8,128)}, u32[]{:S(2)}) copy-start(f32[32,128]{1,0:T(8,128)} %get-tuple-element.32.hot_ref) | copy-start | bytes 49156
  44.8 4.5 %collective-permute-start.15 = (bf16[20,896]{1,0:T(8,128)(2,1)S(1)}, bf16[20,896]{1,0:T(8,128)(2,1)S(1)}, u32[]{:S(2)}, u32[]{:S(2)}) collective-permute-start(bf16[20,896]{1,0:T(8,128)(2,1)S(1)} %get-tuple-element.52), channel_id=1, source_target_pairs={{0,8},{2,10},{4,12},{6,14},{8,0},{10,2},{12,4},{14,6},{16,24},{18,... | collective-permute-start | bytes 107528 | tf_op jit(solution)/shard_map/ppermute | solution.py:271
  46.1 5.8 %collective-permute-start.16 = (bf16[20,896]{1,0:T(8,128)(2,1)S(1)}, bf16[20,896]{1,0:T(8,128)(2,1)S(1)}, u32[]{:S(2)}, u32[]{:S(2)}) collective-permute-start(bf16[20,896]{1,0:T(8,128)(2,1)S(1)} %get-tuple-element.53), channel_id=1, source_target_pairs={{0,16},{2,18},{4,20},{6,22},{8,24},{10,26},{12,28},{14,30},{16,0},... | collective-permute-start | bytes 107528 | tf_op jit(solution)/shard_map/ppermute | solution.py:271
  47.8 5.8 %collective-permute-start.17 = (bf16[20,896]{1,0:T(8,128)(2,1)S(1)}, bf16[20,896]{1,0:T(8,128)(2,1)S(1)}, u32[]{:S(2)}, u32[]{:S(2)}) collective-permute-start(bf16[20,896]{1,0:T(8,128)(2,1)S(1)} %get-tuple-element.54), channel_id=1, source_target_pairs={{0,24},{2,26},{4,28},{6,30},{8,16},{10,18},{12,20},{14,22},{16,8},... | collective-permute-start | bytes 107528 | tf_op jit(solution)/shard_map/ppermute | solution.py:271
  53.9 1.4 %collective-permute-start.18 = (bf16[32,1792]{1,0:T(8,128)(2,1)S(1)}, bf16[32,1792]{1,0:T(8,128)(2,1)S(1)}, u32[]{:S(2)}, u32[]{:S(2)}) collective-permute-start(bf16[32,1792]{1,0:T(8,128)(2,1)S(1)} %get-tuple-element.56), channel_id=1, source_target_pairs={{0,1},{1,0},{2,3},{3,2},{4,5},{5,4},{6,7},{7,6},{8,9},{9,8},{10,11... | collective-permute-start | bytes 344072 | tf_op jit(solution)/shard_map/ppermute | solution.py:267

commit v2 on v1

--- a/solution.py
+++ b/solution.py
@@ -1,3 +1,5 @@
+import functools
+
 import jax
 import jax.numpy as jnp
 from jax import lax
@@ -11,6 +13,7 @@
 SIDES = 2
 CORES = 2
 GROUPS = 2
+FIRST_BLOCKS = 3
 FOLDS = 2
 FIRST_MIB = 60
 CHUNKS = 7
@@ -53,6 +56,10 @@
     return hot, gate
 
 
+def hop(d, live):
+    return (live - d) % live if isinstance(d, int) else lax.rem(live - d, live)
+
+
 def near(k, core):
     if isinstance(core, int):
         return 3 - k if core and k in (1, 2) else k
@@ -72,12 +79,12 @@
     routes, keep, gates = routes_ref[...], keep_ref[...], gates_ref[...]
 
     row = iota((live * 8, 1), 0)
-    expert, slot = place ^ (row // 8), lax.rem(row, 8)
+    expert, slot = place ^ hop(row // 8, live), lax.rem(row, 8)
     hot, _ = pick_rows(routes, keep, gates, expert, slot, slot < MOST)
     outs[2][...] = hot.astype(F32)
 
     row = iota((live * SIDES * MOST, 1), 0)
-    expert = place ^ (row // (SIDES * MOST))
+    expert = place ^ hop(row // (SIDES * MOST), live)
     side, slot = lax.rem(row // MOST, SIDES), lax.rem(row, MOST)
     hot, gate = pick_rows(routes, keep, gates, expert, slot, row >= 0)
     hot_x = (hot & (side == 0)).astype(F32).astype(BF16)
@@ -125,16 +132,19 @@
         out_ref[:, f * fold : (f + 1) * fold] = picked.astype(BF16)
 
 
-def partial_kernel(*refs):
-    blocks, (gate_ref, up_ref, down_ref, out_ref), sided = refs[:SPLIT], refs[SPLIT:-2], refs[-2:]
+def partial_kernel(swap, *refs):
+    (gate_ref, up_ref, down_ref, out_ref), sided = refs[-6:-2], refs[-2:]
+    blocks = [ref[...] for ref in refs[:-6]]
     each, width = blocks[0].shape[0], gate_ref.shape[1]
-    rows = each // SIDES
-    stacked = jnp.concatenate([block[...] for block in blocks], axis=0)
-    at = iota((SPLIT * rows, 1), 0)
-    block = near(at // rows, lax.axis_index("dp"))
+    rows, count = each // SIDES, len(blocks)
+    stacked = jnp.concatenate(blocks, axis=0)
+    at = iota((count * rows, 1), 0)
+    block = at // rows
+    if swap:
+        block = near(block, lax.axis_index("dp"))
     for side in range(SIDES):
         wanted = block * each + side * rows + lax.rem(at, rows)
-        sided[side][...] = dot(one_hot(wanted, SPLIT * each), stacked).astype(BF16)
+        sided[side][...] = dot(one_hot(wanted, count * each), stacked).astype(BF16)
     out_ref[:, :width] = dot(sided[0][...], gate_ref[...])
     out_ref[:, width : 2 * width] = dot(sided[0][...], up_ref[...])
     out_ref[:, 2 * width :] = dot(sided[1][...], down_ref[...])
@@ -158,14 +168,12 @@
     sides_ref[:, width : 2 * width] = up_side
     sides_ref[:, 2 * width :] = (activated * pre_up).astype(BF16)
     across = ((1,), (1,))
-    at = iota((SPLIT * rows, 1), 0)
-    k = near(at // rows, lax.axis_index("dp"))
-    group, row = lax.rem(at, rows) // (rows // GROUPS), lax.rem(at, rows // GROUPS)
-    order = one_hot(((GROUPS - 1 - group) * SPLIT + k) * (rows // GROUPS) + row, SPLIT * rows)
-    gate_side, up_side = dot(order, gate_side).astype(BF16), dot(order, up_side).astype(BF16)
     part = (dot(gate_side, gate_ref[...], across) + dot(up_side, up_ref[...], across)).astype(BF16)
-    for k in range(SPLIT):
-        parts[k][...] = part[k * rows : (k + 1) * rows]
+    swapped = lax.axis_index("dp") == 1
+    parts[0][...] = part[:rows]
+    parts[1][...] = jnp.where(swapped, part[2 * rows : 3 * rows], part[rows : 2 * rows])
+    parts[2][...] = jnp.where(swapped, part[rows : 2 * rows], part[2 * rows : 3 * rows])
+    parts[3][...] = part[3 * rows :]
 
 
 def grads_kernel(*refs):
@@ -267,15 +275,15 @@
         return lax.ppermute(array, "dp", [(r, r ^ 1) for r in range(CORES)])
 
     def along_z(array, d):
-        hop = [(i, (i // SPLIT ^ d) * SPLIT + i % SPLIT) for i in range(devices)]
-        return lax.ppermute(array, "expert", hop)
+        moves = [(i, (i // SPLIT ^ hop(d, live)) * SPLIT + i % SPLIT) for i in range(devices)]
+        return lax.ppermute(array, "expert", moves)
 
     def in_plane(array, k):
-        hop = []
+        moves = []
         for i in range(devices):
             for r in range(CORES):
-                hop.append((i * CORES + r, (i ^ near(k, r)) * CORES + r))
-        return lax.ppermute(array, ("expert", "dp"), hop)
+                moves.append((i * CORES + r, (i ^ near(k, r)) * CORES + r))
+        return lax.ppermute(array, ("expert", "dp"), moves)
 
     gathered = like((live * SIDES * MOST, half), BF16)
     mine, other, hot = pl.pallas_call(
@@ -303,25 +311,18 @@
         2e7,
     )
     chunks = [chunks[0]] + [along_z(chunks[d], d) for d in range(1, live)]
+    own = call(merge_kernel, "merge_rows", like((SIDES * rows, half), BF16), chunks, 1e8, 1e6)
+    first, second = in_plane(own, 1), in_plane(own, 2)
+    blocks = [own, first, second, in_plane(first, 2)]
     mines, others, xs, ss = [], [], [], []
-    rows_in_group, planes = total // GROUPS, live // GROUPS
-    for group in reversed(range(GROUPS)):
-        rows_here = call(
-            merge_kernel,
-            "merge_rows",
-            like((SIDES * rows // GROUPS, half), BF16),
-            chunks[group * planes : (group + 1) * planes],
-            1e8,
-            1e6,
-        )
-        first, second = in_plane(rows_here, 1), in_plane(rows_here, 2)
-        across = in_plane(first, 2)
+    for group in (blocks[:FIRST_BLOCKS], blocks[FIRST_BLOCKS:]):
+        count = len(group) * rows
         mine, x, s = call(
-            partial_kernel,
+            functools.partial(partial_kernel, len(group) == FIRST_BLOCKS),
             "partial_products",
-            [like((rows_in_group, 3 * width), F32)] + [like((rows_in_group, half), BF16)] * SIDES,
-            [rows_here, first, second, across, gate_weight, up_weight, down_transposed],
-            6 * rows_in_group * half * width,
+            [like((count, 3 * width), F32)] + [like((count, half), BF16)] * SIDES,
+            [*group, gate_weight, up_weight, down_transposed],
+            (1 if len(group) == FIRST_BLOCKS else 16) * 6 * count * half * width,
             6 * half * width,
         )
         mines.append(mine)
@@ -337,7 +338,7 @@
         4 * half * width,
     )
     parts, sides = sided[:SPLIT], sided[SPLIT]
-    parts = [parts[0]] + [in_plane(parts[k], k) for k in range(1, SPLIT)]
+    parts = [parts[0]] + [in_plane(parts[k], k) for k in reversed(range(1, SPLIT))]
     gate_grad, up_grad, down_grad, token = pl.pallas_call(
         grads_kernel,
         out_shape=[like((half, width), BF16)] * 3 + [like((8, 128), F32)],

time: 56.8 us -> 58.5 us (1.030)
  waiting for transfers between devices: 21 us -> 28.3 us
  starting transfers between devices: 22.7 us -> 17.7 us
  Pallas kernels: 11.2 us -> 10.6 us
    ppermute x15 -> x12, waiting for transfers between devices: 16.8 us -> 24.3 us  [the longest x6 15.6 us: in_plane(): return lax.ppermute(array, ('expert', 'dp'), moves)]
    ppermute x15 -> x12, starting transfers between devices: 22 us -> 17 us  [the longest x6 10.1 us: along_z(): return lax.ppermute(array, 'expert', moves)]
    pallas_call x9 -> x8, Pallas kernels: 6.1 us -> 5.52 us  [call(): pl.pallas_call(kernel, out_shape=out_shape, in_specs=[vmem] * len(operand...]
  transfers between devices with their start and end apart: 19 -> 16, of which waited for: 13 -> 11; matrix products, arithmetic and copies ran while one was open for 0% -> 0% of each run, Pallas kernels for 9% -> 8%
where the time goes in v2:
time: 58.5 us; the launch traced here: 58.3 us
  waiting for transfers between devices  28.3 us (48%)
  starting transfers between devices  17.7 us (30%)
  Pallas kernels  10.6 us (18%)
  local copies, waits for them, and re-layouts  0.92 us (2%)
  between operations  0.76 us (1%)
    ppermute x6, waiting for transfers between devices, in_plane(): return lax.ppermute(array, ('expert', 'dp'), moves)  15.6 us
    ppermute x6, starting transfers between devices, along_z(): return lax.ppermute(array, 'expert', moves)  10.1 us
    ppermute x6, waiting for transfers between devices, along_z(): return lax.ppermute(array, 'expert', moves)  8.72 us
    ppermute x6, starting transfers between devices, in_plane(): return lax.ppermute(array, ('expert', 'dp'), moves)  6.89 us
    pallas_call x8, Pallas kernels, call(): pl.pallas_call(kernel, out_shape=out_shape, in_specs=[vmem] * len(operand...  5.52 us
    ppermute x4, waiting for transfers between devices, swap_cores(): return lax.ppermute(array, 'dp', [(r, r ^ 1) for r in range(CORES)])  3.94 us
    pallas_call x1, Pallas kernels, body(): pl.pallas_call(lambda *refs: gather_kernel(live, *refs), out_shape=[gathe...  2.6 us
    pallas_call x1, Pallas kernels, body(): pl.pallas_call(grads_kernel, out_shape=[like((half, width), BF16)] * 3 +...  2.51 us
  transfers between devices with their start and end apart: 16, of which 11 were waited for; matrix products, arithmetic and copies ran while one was open for 0% of the time, Pallas kernels for 8%

profile of v2, /device:TPU:0, one launch (start us, length us, event | category | flops | bytes accessed | tf_op | source)
XLA Modules:
  0.0 58.3 jit_solution(9813424883116694596)
XLA Ops:
  0.6 2.6 %gather_rows.1 = (bf16[40,1792]{1,0:T(8,128)(2,1)}, bf16[40,1792]{1,0:T(8,128)(2,1)}, f32[32,128]{1,0:T(8,128)}) custom-call(s32[8,128]{1,0:T(8,128)} %bitcast.3, s32[8,128]{1,0:T(8,128)} %bitcast.4, f32[8,128]{1,0:T(8,128)} %bitcast.5, bf16[128,3584]{1,0:T(8,128)(2,1)} %refs_3_.3, bf16[128,3584]{1,0:T(8,128)(2,1)} %refs_4_.3), custom_call_target="tpu_custom_call" | custom-call | tf_op jit(solution)/shard_map/gather_rows/pallas_call | solution.py:289
  3.2 0.5 collective-permute-start
  3.8 1.2 %collective-permute-done.refs_1_ = bf16[40,1792]{1,0:T(8,128)(2,1)S(1)} collective-permute-done((bf16[40,1792]{1,0:T(8,128)(2,1)}, bf16[40,1792]{1,0:T(8,128)(2,1)S(1)}, u32[]{:S(2)}, u32[]{:S(2)}) %collective-permute-start) | collective-permute-done | bytes 143392 | tf_op jit(solution)/shard_map/ppermute | solution.py:275
  5.0 0.0 copy-start.4
  5.0 0.9 %copy-done.4 = bf16[40,1792]{1,0:T(8,128)(2,1)S(1)} copy-done((bf16[40,1792]{1,0:T(8,128)(2,1)S(1)}, bf16[40,1792]{1,0:T(8,128)(2,1)}, u32[]{:S(2)}) %copy-start.4) | copy-done | bytes 143384
  5.9 0.0 copy-start
  5.9 0.0 copy-start.1
  5.9 0.0 copy-start.2
  5.9 0.4 chunk_rows.1
  6.3 5.0 %collective-permute-start.1 = (bf16[40,896]{1,0:T(8,128)(2,1)S(1)}, bf16[40,896]{1,0:T(8,128)(2,1)S(1)}, u32[]{:S(2)}, u32[]{:S(2)}) collective-permute-start(bf16[40,896]{1,0:T(8,128)(2,1)S(1)} %get-tuple-element.36), channel_id=1, source_target_pairs={{0,24},{2,26},{4,28},{6,30},{8,16},{10,18},{12,20},{14,22},{16,8},... | collective-permute-start | bytes 215048 | tf_op jit(solution)/shard_map/ppermute | solution.py:279
  11.3 0.0 collective-permute-start.2
  11.3 0.6 %collective-permute-start.3 = (bf16[40,896]{1,0:T(8,128)(2,1)S(1)}, bf16[40,896]{1,0:T(8,128)(2,1)S(1)}, u32[]{:S(2)}, u32[]{:S(2)}) collective-permute-start(bf16[40,896]{1,0:T(8,128)(2,1)S(1)} %get-tuple-element.38), channel_id=1, source_target_pairs={{0,8},{2,10},{4,12},{6,14},{8,0},{10,2},{12,4},{14,6},{16,24},{18,... | collective-permute-start | bytes 215048 | tf_op jit(solution)/shard_map/ppermute | solution.py:279
  11.9 2.3 %collective-permute-done.1.refs_1_ = bf16[40,896]{1,0:T(8,128)(2,1)S(1)} collective-permute-done((bf16[40,896]{1,0:T(8,128)(2,1)S(1)}, bf16[40,896]{1,0:T(8,128)(2,1)S(1)}, u32[]{:S(2)}, u32[]{:S(2)}) %collective-permute-start.1) | collective-permute-done | bytes 71712 | tf_op jit(solution)/shard_map/ppermute | solution.py:279
  14.2 3.4 %collective-permute-done.2.refs_2_ = bf16[40,896]{1,0:T(8,128)(2,1)S(1)} collective-permute-done((bf16[40,896]{1,0:T(8,128)(2,1)S(1)}, bf16[40,896]{1,0:T(8,128)(2,1)S(1)}, u32[]{:S(2)}, u32[]{:S(2)}) %collective-permute-start.2) | collective-permute-done | bytes 71712 | tf_op jit(solution)/shard_map/ppermute | solution.py:279
  17.6 0.0 collective-permute-done.3.refs_3_
  17.6 0.3 merge_rows.1.refs_0_
  17.9 1.6 %collective-permute-start.4 = (bf16[80,1792]{1,0:T(8,128)(2,1)S(1)}, bf16[80,1792]{1,0:T(8,128)(2,1)S(1)}, u32[]{:S(2)}, u32[]{:S(2)}) collective-permute-start(bf16[80,1792]{1,0:T(8,128)(2,1)S(1)} %merge_rows.1.refs_0_), channel_id=1, source_target_pairs={{0,2},{1,5},{2,0},{3,7},{4,6},{5,1},{6,4},{7,3},{8,10},{9,13},{10,... | collective-permute-start | bytes 860168 | tf_op jit(solution)/shard_map/ppermute | solution.py:286
  19.5 1.5 %collective-permute-start.5 = (bf16[80,1792]{1,0:T(8,128)(2,1)S(1)}, bf16[80,1792]{1,0:T(8,128)(2,1)S(1)}, u32[]{:S(2)}, u32[]{:S(2)}) collective-permute-start(bf16[80,1792]{1,0:T(8,128)(2,1)S(1)} %merge_rows.1.refs_0_), channel_id=1, source_target_pairs={{0,4},{1,3},{2,6},{3,1},{4,0},{5,7},{6,2},{7,5},{8,12},{9,11},{10,... | collective-permute-start | bytes 860168 | tf_op jit(solution)/shard_map/ppermute | solution.py:286
  21.0 6.7 %collective-permute-done.4.refs_1_ = bf16[80,1792]{1,0:T(8,128)(2,1)S(1)} collective-permute-done((bf16[80,1792]{1,0:T(8,128)(2,1)S(1)}, bf16[80,1792]{1,0:T(8,128)(2,1)S(1)}, u32[]{:S(2)}, u32[]{:S(2)}) %collective-permute-start.4) | collective-permute-done | bytes 286752 | tf_op jit(solution)/shard_map/ppermute | solution.py:286
  27.7 0.3 collective-permute-start.6
  28.0 0.0 collective-permute-done.5.refs_2_
  28.0 0.0 copy-done
  28.0 0.0 copy-done.1
  28.0 0.0 copy-done.2
  28.0 1.1 %partial_products.2 = (f32[120,1152]{1,0:T(8,128)S(1)}, bf16[120,1792]{1,0:T(8,128)(2,1)S(1)}, bf16[120,1792]{1,0:T(8,128)(2,1)S(1)}) custom-call(bf16[80,1792]{1,0:T(8,128)(2,1)S(1)} %merge_rows.1.refs_0_, bf16[80,1792]{1,0:T(8,128)(2,1)S(1)} %collective-permute-done.4.refs_1_, bf16[80,1792]{1,0:T(8,128)(2,1)S(1)} %collective-permute-done.5.refs_2_, ...), custom_call_target="tpu_custom_call" | custom-call | flops 495452160 | bytes 4128768 | tf_op jit(solution)/shard_map/partial_products/pallas_call | solution.py:264
  29.1 0.1 collective-permute-start.7
  29.2 5.1 %collective-permute-done.6.refs_0_ = bf16[80,1792]{1,0:T(8,128)(2,1)S(1)} collective-permute-done((bf16[80,1792]{1,0:T(8,128)(2,1)S(1)}, bf16[80,1792]{1,0:T(8,128)(2,1)S(1)}, u32[]{:S(2)}, u32[]{:S(2)}) %collective-permute-start.6) | collective-permute-done | bytes 286752 | tf_op jit(solution)/shard_map/ppermute | solution.py:286
  34.4 0.9 %partial_products.3 = (f32[40,1152]{1,0:T(8,128)S(1)}, bf16[40,1792]{1,0:T(8,128)(2,1)S(1)}, bf16[40,1792]{1,0:T(8,128)(2,1)S(1)}) custom-call(bf16[80,1792]{1,0:T(8,128)(2,1)S(1)} %collective-permute-done.6.refs_0_, bf16[1792,384]{1,0:T(8,128)(2,1)S(1)} %copy-done, bf16[1792,384]{1,0:T(8,128)(2,1)S(1)} %copy-done.1, bf16[1792,384]{1,0:T(8,128)(2,1)S(1)} %copy-done.2), custom_call_target="tpu_custom_call" | custom-call | flops 2642411520 | bytes 4128768 | tf_op jit(solution)/shard_map/partial_products/pallas_call | solution.py:264
  35.2 0.1 collective-permute-start.8
  35.3 1.4 %collective-permute-done.8.refs_3_ = f32[40,1152]{1,0:T(8,128)S(1)} collective-permute-done((f32[40,1152]{1,0:T(8,128)S(1)}, f32[40,1152]{1,0:T(8,128)S(1)}, u32[]{:S(2)}, u32[]{:S(2)}) %collective-permute-start.8) | collective-permute-done | bytes 184352 | tf_op jit(solution)/shard_map/ppermute | solution.py:275
  36.7 0.0 collective-permute-done.7.refs_2_
  36.7 1.0 %sides_and_parts.1 = (bf16[40,1792]{1,0:T(8,128)(2,1)S(1)}, bf16[40,1792]{1,0:T(8,128)(2,1)S(1)}, bf16[40,1792]{1,0:T(8,128)(2,1)S(1)}, bf16[40,1792]{1,0:T(8,128)(2,1)S(1)}, bf16[160,1152]{1,0:T(8,128)(2,1)S(1)}) custom-call(f32[120,1152]{1,0:T(8,128)S(1)} %get-tuple-element.39.refs_0_, f32[40,1152]{1,0:T(8,128)S(1)} %get-tuple-element.40.refs_1_, ...), custom_call_target="tpu_custom_call" | custom-call | flops 440401920 | bytes 2752512 | tf_op jit(solution)/shard_map/sides_and_parts/pallas_call | solution.py:264
  37.7 1.2 %collective-permute-start.9 = (bf16[40,1792]{1,0:T(8,128)(2,1)S(1)}, bf16[40,1792]{1,0:T(8,128)(2,1)S(1)}, u32[]{:S(2)}, u32[]{:S(2)}) collective-permute-start(bf16[40,1792]{1,0:T(8,128)(2,1)S(1)} %get-tuple-element.42), channel_id=1, source_target_pairs={{0,6},{1,7},{2,4},{3,5},{4,2},{5,3},{6,0},{7,1},{8,14},{9,15},{10,... | collective-permute-start | bytes 430088 | tf_op jit(solution)/shard_map/ppermute | solution.py:286
  39.0 1.8 %collective-permute-start.10 = (bf16[40,1792]{1,0:T(8,128)(2,1)S(1)}, bf16[40,1792]{1,0:T(8,128)(2,1)S(1)}, u32[]{:S(2)}, u32[]{:S(2)}) collective-permute-start(bf16[40,1792]{1,0:T(8,128)(2,1)S(1)} %get-tuple-element.43), channel_id=1, source_target_pairs={{0,4},{1,3},{2,6},{3,1},{4,0},{5,7},{6,2},{7,5},{8,12},{9,11},{10,... | collective-permute-start | bytes 430088 | tf_op jit(solution)/shard_map/ppermute | solution.py:286
  40.7 0.5 collective-permute-start.11
  41.3 0.0 copy-start.3
  41.3 2.5 %weight_grads.1 = (bf16[1792,384]{1,0:T(8,128)(2,1)}, bf16[1792,384]{1,0:T(8,128)(2,1)}, bf16[1792,384]{1,0:T(8,128)(2,1)}, f32[8,128]{1,0:T(8,128)S(1)}) custom-call(bf16[120,1792]{1,0:T(8,128)(2,1)S(1)} %get-tuple-element.45.refs_0_, bf16[40,1792]{1,0:T(8,128)(2,1)S(1)} %get-tuple-element.46.refs_1_, bf16[120,1792]{1,0:T(8,128)(2,1)S(1)} %get-tuple-element.47.refs_2_, ...), custom_call_target="tpu_custom_call" | custom-call | flops 660602880 | bytes 5275648 | tf_op jit(solution)/shard_map/weight_grads/pallas_call | solution.py:342
  43.8 1.5 %collective-permute-done.9.refs_1_ = bf16[40,1792]{1,0:T(8,128)(2,1)S(1)} collective-permute-done((bf16[40,1792]{1,0:T(8,128)(2,1)S(1)}, bf16[40,1792]{1,0:T(8,128)(2,1)S(1)}, u32[]{:S(2)}, u32[]{:S(2)}) %collective-permute-start.9) | collective-permute-done | bytes 143392 | tf_op jit(solution)/shard_map/ppermute | solution.py:286
  45.3 2.2 %collective-permute-done.10.refs_2_ = bf16[40,1792]{1,0:T(8,128)(2,1)S(1)} collective-permute-done((bf16[40,1792]{1,0:T(8,128)(2,1)S(1)}, bf16[40,1792]{1,0:T(8,128)(2,1)S(1)}, u32[]{:S(2)}, u32[]{:S(2)}) %collective-permute-start.10) | collective-permute-done | bytes 143392 | tf_op jit(solution)/shard_map/ppermute | solution.py:286
  47.6 0.0 collective-permute-done.11.refs_3_
  47.6 0.3 sum_parts.1
  47.9 2.5 %collective-permute-start.12 = (bf16[20,896]{1,0:T(8,128)(2,1)S(1)}, bf16[20,896]{1,0:T(8,128)(2,1)S(1)}, u32[]{:S(2)}, u32[]{:S(2)}) collective-permute-start(bf16[20,896]{1,0:T(8,128)(2,1)S(1)} %get-tuple-element.52), channel_id=1, source_target_pairs={{0,24},{2,26},{4,28},{6,30},{8,16},{10,18},{12,20},{14,22},{16,8},... | collective-permute-start | bytes 107528 | tf_op jit(solution)/shard_map/ppermute | solution.py:279
  50.4 0.0 collective-permute-start.13
  50.4 1.9 %collective-permute-start.14 = (bf16[20,896]{1,0:T(8,128)(2,1)S(1)}, bf16[20,896]{1,0:T(8,128)(2,1)S(1)}, u32[]{:S(2)}, u32[]{:S(2)}) collective-permute-start(bf16[20,896]{1,0:T(8,128)(2,1)S(1)} %get-tuple-element.54), channel_id=1, source_target_pairs={{0,8},{2,10},{4,12},{6,14},{8,0},{10,2},{12,4},{14,6},{16,24},{18,... | collective-permute-start | bytes 107528 | tf_op jit(solution)/shard_map/ppermute | solution.py:279
  52.3 1.5 %collective-permute-done.12.refs_1_ = bf16[20,896]{1,0:T(8,128)(2,1)S(1)} collective-permute-done((bf16[20,896]{1,0:T(8,128)(2,1)S(1)}, bf16[20,896]{1,0:T(8,128)(2,1)S(1)}, u32[]{:S(2)}, u32[]{:S(2)}) %collective-permute-start.12) | collective-permute-done | bytes 35872 | tf_op jit(solution)/shard_map/ppermute | solution.py:279
  53.8 1.6 %collective-permute-done.13.refs_2_ = bf16[20,896]{1,0:T(8,128)(2,1)S(1)} collective-permute-done((bf16[20,896]{1,0:T(8,128)(2,1)S(1)}, bf16[20,896]{1,0:T(8,128)(2,1)S(1)}, u32[]{:S(2)}, u32[]{:S(2)}) %collective-permute-start.13) | collective-permute-done | bytes 35872 | tf_op jit(solution)/shard_map/ppermute | solution.py:279
  55.3 0.0 collective-permute-done.14.refs_3_
  55.3 0.2 split_rows.1
  55.6 0.1 collective-permute-start.15
  55.6 1.3 %collective-permute-done.15.other_ref = bf16[32,1792]{1,0:T(8,128)(2,1)S(1)} collective-permute-done((bf16[32,1792]{1,0:T(8,128)(2,1)S(1)}, bf16[32,1792]{1,0:T(8,128)(2,1)S(1)}, u32[]{:S(2)}, u32[]{:S(2)}) %collective-permute-start.15) | collective-permute-done | bytes 114720 | tf_op jit(solution)/shard_map/ppermute | solution.py:275
  57.0 0.0 copy-done.3
  57.0 1.3 %place_rows.1 = bf16[128,3584]{1,0:T(8,128)(2,1)} custom-call(f32[32,128]{1,0:T(8,128)S(1)} %copy-done.3, bf16[32,1792]{1,0:T(8,128)(2,1)S(1)} %get-tuple-element.55.mine_ref, bf16[32,1792]{1,0:T(8,128)(2,1)S(1)} %collective-permute-done.15.other_ref), custom_call_target="tpu_custom_call" | custom-call | tf_op jit(solution)/shard_map/place_rows/pallas_call | solution.py:264
Async XLA Ops:
  3.2 1.7 %collective-permute-start = (bf16[40,1792]{1,0:T(8,128)(2,1)}, bf16[40,1792]{1,0:T(8,128)(2,1)S(1)}, u32[]{:S(2)}, u32[]{:S(2)}) collective-permute-start(bf16[40,1792]{1,0:T(8,128)(2,1)} %get-tuple-element.34), channel_id=1, source_target_pairs={{0,1},{1,0},{2,3},{3,2},{4,5},{5,4},{6,7},{7,6},{8,9},{9,8},{10,11... | collective-permute-start | bytes 430088 | tf_op jit(solution)/shard_map/ppermute | solution.py:275
  5.0 0.9 %copy-start.4 = (bf16[40,1792]{1,0:T(8,128)(2,1)S(1)}, bf16[40,1792]{1,0:T(8,128)(2,1)}, u32[]{:S(2)}) copy-start(bf16[40,1792]{1,0:T(8,128)(2,1)} %get-tuple-element.33.refs_0_) | copy-start | bytes 430084
  5.9 22.1 %copy-start = (bf16[1792,384]{1,0:T(8,128)(2,1)S(1)}, bf16[1792,384]{1,0:T(8,128)(2,1)}, u32[]{:S(2)}) copy-start(bf16[1792,384]{1,0:T(8,128)(2,1)} %refs_4_.5) | copy-start | bytes 4128772
  5.9 22.1 %copy-start.1 = (bf16[1792,384]{1,0:T(8,128)(2,1)S(1)}, bf16[1792,384]{1,0:T(8,128)(2,1)}, u32[]{:S(2)}) copy-start(bf16[1792,384]{1,0:T(8,128)(2,1)} %refs_5_.3) | copy-start | bytes 4128772
  5.9 22.1 %copy-start.2 = (bf16[1792,384]{1,0:T(8,128)(2,1)S(1)}, bf16[1792,384]{1,0:T(8,128)(2,1)}, u32[]{:S(2)}) copy-start(bf16[1792,384]{1,0:T(8,128)(2,1)} %refs_3_.5) | copy-start | bytes 4128772
  6.3 7.9 %collective-permute-start.1 = (bf16[40,896]{1,0:T(8,128)(2,1)S(1)}, bf16[40,896]{1,0:T(8,128)(2,1)S(1)}, u32[]{:S(2)}, u32[]{:S(2)}) collective-permute-start(bf16[40,896]{1,0:T(8,128)(2,1)S(1)} %get-tuple-element.36), channel_id=1, source_target_pairs={{0,24},{2,26},{4,28},{6,30},{8,16},{10,18},{12,20},{14,22},{16,8},... | collective-permute-start | bytes 215048 | tf_op jit(solution)/shard_map/ppermute | solution.py:279
  11.3 6.3 %collective-permute-start.2 = (bf16[40,896]{1,0:T(8,128)(2,1)S(1)}, bf16[40,896]{1,0:T(8,128)(2,1)S(1)}, u32[]{:S(2)}, u32[]{:S(2)}) collective-permute-start(bf16[40,896]{1,0:T(8,128)(2,1)S(1)} %get-tuple-element.37), channel_id=1, source_target_pairs={{0,16},{2,18},{4,20},{6,22},{8,24},{10,26},{12,28},{14,30},{16,0},... | collective-permute-start | bytes 215048 | tf_op jit(solution)/shard_map/ppermute | solution.py:279
  11.3 6.3 %collective-permute-start.3 = (bf16[40,896]{1,0:T(8,128)(2,1)S(1)}, bf16[40,896]{1,0:T(8,128)(2,1)S(1)}, u32[]{:S(2)}, u32[]{:S(2)}) collective-permute-start(bf16[40,896]{1,0:T(8,128)(2,1)S(1)} %get-tuple-element.38), channel_id=1, source_target_pairs={{0,8},{2,10},{4,12},{6,14},{8,0},{10,2},{12,4},{14,6},{16,24},{18,... | collective-permute-start | bytes 215048 | tf_op jit(solution)/shard_map/ppermute | solution.py:279
  17.9 9.8 %collective-permute-start.4 = (bf16[80,1792]{1,0:T(8,128)(2,1)S(1)}, bf16[80,1792]{1,0:T(8,128)(2,1)S(1)}, u32[]{:S(2)}, u32[]{:S(2)}) collective-permute-start(bf16[80,1792]{1,0:T(8,128)(2,1)S(1)} %merge_rows.1.refs_0_), channel_id=1, source_target_pairs={{0,2},{1,5},{2,0},{3,7},{4,6},{5,1},{6,4},{7,3},{8,10},{9,13},{10,... | collective-permute-start | bytes 860168 | tf_op jit(solution)/shard_map/ppermute | solution.py:286
  19.5 8.5 %collective-permute-start.5 = (bf16[80,1792]{1,0:T(8,128)(2,1)S(1)}, bf16[80,1792]{1,0:T(8,128)(2,1)S(1)}, u32[]{:S(2)}, u32[]{:S(2)}) collective-permute-start(bf16[80,1792]{1,0:T(8,128)(2,1)S(1)} %merge_rows.1.refs_0_), channel_id=1, source_target_pairs={{0,4},{1,3},{2,6},{3,1},{4,0},{5,7},{6,2},{7,5},{8,12},{9,11},{10,... | collective-permute-start | bytes 860168 | tf_op jit(solution)/shard_map/ppermute | solution.py:286
  27.7 6.6 %collective-permute-start.6 = (bf16[80,1792]{1,0:T(8,128)(2,1)S(1)}, bf16[80,1792]{1,0:T(8,128)(2,1)S(1)}, u32[]{:S(2)}, u32[]{:S(2)}) collective-permute-start(bf16[80,1792]{1,0:T(8,128)(2,1)S(1)} %collective-permute-done.4.refs_1_), channel_id=1, source_target_pairs={{0,4},{1,3},{2,6},{3,1},{4,0},{5,7},{6,2},{7,5},{8,12},{9,11},{10,... | collective-permute-start | bytes 860168 | tf_op jit(solution)/shard_map/ppermute | solution.py:286
  29.1 7.6 %collective-permute-start.7 = (f32[120,1152]{1,0:T(8,128)S(1)}, f32[120,1152]{1,0:T(8,128)S(1)}, u32[]{:S(2)}, u32[]{:S(2)}) collective-permute-start(f32[120,1152]{1,0:T(8,128)S(1)} %get-tuple-element.39.refs_0_), channel_id=1, source_target_pairs={{0,1},{1,0},{2,3},{3,2},{4,5},{5,4},{6,7},{7,6},{8,9},{9,8},{10,11... | collective-permute-start | bytes 1658888 | tf_op jit(solution)/shard_map/ppermute | solution.py:275
  35.2 1.5 %collective-permute-start.8 = (f32[40,1152]{1,0:T(8,128)S(1)}, f32[40,1152]{1,0:T(8,128)S(1)}, u32[]{:S(2)}, u32[]{:S(2)}) collective-permute-start(f32[40,1152]{1,0:T(8,128)S(1)} %get-tuple-element.40.refs_1_), channel_id=1, source_target_pairs={{0,1},{1,0},{2,3},{3,2},{4,5},{5,4},{6,7},{7,6},{8,9},{9,8},{10,11... | collective-permute-start | bytes 552968 | tf_op jit(solution)/shard_map/ppermute | solution.py:275
  37.7 7.6 %collective-permute-start.9 = (bf16[40,1792]{1,0:T(8,128)(2,1)S(1)}, bf16[40,1792]{1,0:T(8,128)(2,1)S(1)}, u32[]{:S(2)}, u32[]{:S(2)}) collective-permute-start(bf16[40,1792]{1,0:T(8,128)(2,1)S(1)} %get-tuple-element.42), channel_id=1, source_target_pairs={{0,6},{1,7},{2,4},{3,5},{4,2},{5,3},{6,0},{7,1},{8,14},{9,15},{10,... | collective-permute-start | bytes 430088 | tf_op jit(solution)/shard_map/ppermute | solution.py:286
  39.0 8.6 %collective-permute-start.10 = (bf16[40,1792]{1,0:T(8,128)(2,1)S(1)}, bf16[40,1792]{1,0:T(8,128)(2,1)S(1)}, u32[]{:S(2)}, u32[]{:S(2)}) collective-permute-start(bf16[40,1792]{1,0:T(8,128)(2,1)S(1)} %get-tuple-element.43), channel_id=1, source_target_pairs={{0,4},{1,3},{2,6},{3,1},{4,0},{5,7},{6,2},{7,5},{8,12},{9,11},{10,... | collective-permute-start | bytes 430088 | tf_op jit(solution)/shard_map/ppermute | solution.py:286
  40.7 6.8 %collective-permute-start.11 = (bf16[40,1792]{1,0:T(8,128)(2,1)S(1)}, bf16[40,1792]{1,0:T(8,128)(2,1)S(1)}, u32[]{:S(2)}, u32[]{:S(2)}) collective-permute-start(bf16[40,1792]{1,0:T(8,128)(2,1)S(1)} %get-tuple-element.44), channel_id=1, source_target_pairs={{0,2},{1,5},{2,0},{3,7},{4,6},{5,1},{6,4},{7,3},{8,10},{9,13},{10,... | collective-permute-start | bytes 430088 | tf_op jit(solution)/shard_map/ppermute | solution.py:286
  41.3 15.7 %copy-start.3 = (f32[32,128]{1,0:T(8,128)S(1)}, f32[32,128]{1,0:T(8,128)}, u32[]{:S(2)}) copy-start(f32[32,128]{1,0:T(8,128)} %get-tuple-element.32.hot_ref) | copy-start | bytes 49156
  47.9 5.9 %collective-permute-start.12 = (bf16[20,896]{1,0:T(8,128)(2,1)S(1)}, bf16[20,896]{1,0:T(8,128)(2,1)S(1)}, u32[]{:S(2)}, u32[]{:S(2)}) collective-permute-start(bf16[20,896]{1,0:T(8,128)(2,1)S(1)} %get-tuple-element.52), channel_id=1, source_target_pairs={{0,24},{2,26},{4,28},{6,30},{8,16},{10,18},{12,20},{14,22},{16,8},... | collective-permute-start | bytes 107528 | tf_op jit(solution)/shard_map/ppermute | solution.py:279
  50.4 4.9 %collective-permute-start.13 = (bf16[20,896]{1,0:T(8,128)(2,1)S(1)}, bf16[20,896]{1,0:T(8,128)(2,1)S(1)}, u32[]{:S(2)}, u32[]{:S(2)}) collective-permute-start(bf16[20,896]{1,0:T(8,128)(2,1)S(1)} %get-tuple-element.53), channel_id=1, source_target_pairs={{0,16},{2,18},{4,20},{6,22},{8,24},{10,26},{12,28},{14,30},{16,0},... | collective-permute-start | bytes 107528 | tf_op jit(solution)/shard_map/ppermute | solution.py:279
  50.4 4.9 %collective-permute-start.14 = (bf16[20,896]{1,0:T(8,128)(2,1)S(1)}, bf16[20,896]{1,0:T(8,128)(2,1)S(1)}, u32[]{:S(2)}, u32[]{:S(2)}) collective-permute-start(bf16[20,896]{1,0:T(8,128)(2,1)S(1)} %get-tuple-element.54), channel_id=1, source_target_pairs={{0,8},{2,10},{4,12},{6,14},{8,0},{10,2},{12,4},{14,6},{16,24},{18,... | collective-permute-start | bytes 107528 | tf_op jit(solution)/shard_map/ppermute | solution.py:279
  55.6 1.4 %collective-permute-start.15 = (bf16[32,1792]{1,0:T(8,128)(2,1)S(1)}, bf16[32,1792]{1,0:T(8,128)(2,1)S(1)}, u32[]{:S(2)}, u32[]{:S(2)}) collective-permute-start(bf16[32,1792]{1,0:T(8,128)(2,1)S(1)} %get-tuple-element.56), channel_id=1, source_target_pairs={{0,1},{1,0},{2,3},{3,2},{4,5},{5,4},{6,7},{7,6},{8,9},{9,8},{10,11... | collective-permute-start | bytes 344072 | tf_op jit(solution)/shard_map/ppermute | solution.py:275

commit v3 on v1

--- a/solution.py
+++ b/solution.py
@@ -221,7 +221,7 @@
     out = iota((CORES * rows, 1), 0)
     q, d, slot = out // rows, lax.rem(out, rows) // 8, lax.rem(out, 8)
     for f in range(FOLDS):
-        wanted = d * size + (f * CORES + (q ^ me)) * MOST + slot
+        wanted = lax.rem(live - d, live) * size + (f * CORES + (q ^ me)) * MOST + slot
         picked = dot(one_hot(jnp.where(slot < MOST, wanted, -1), live * size), stacked).astype(BF16)
         for core in range(CORES):
             outs[core][:, f * fold : (f + 1) * fold] = picked[core * rows : (core + 1) * rows]
@@ -305,15 +305,17 @@
     chunks = [chunks[0]] + [along_z(chunks[d], d) for d in range(1, live)]
     mines, others, xs, ss = [], [], [], []
     rows_in_group, planes = total // GROUPS, live // GROUPS
-    for group in reversed(range(GROUPS)):
+    for group in range(GROUPS):
         rows_here = call(
             merge_kernel,
             "merge_rows",
             like((SIDES * rows // GROUPS, half), BF16),
             chunks[group * planes : (group + 1) * planes],
-            1e8,
+            1e10 if group else 1e8,
             1e6,
         )
+        if group:
+            rows_here, _ = lax.optimization_barrier((rows_here, second))
         first, second = in_plane(rows_here, 1), in_plane(rows_here, 2)
         across = in_plane(first, 2)
         mine, x, s = call(
@@ -328,6 +330,7 @@
         others.append(swap_cores(mine))
         xs.append(x)
         ss.append(s)
+    mines, others, xs, ss = mines[::-1], others[::-1], xs[::-1], ss[::-1]
     sided = call(
         sides_kernel,
         "sides_and_parts",
@@ -337,7 +340,7 @@
         4 * half * width,
     )
     parts, sides = sided[:SPLIT], sided[SPLIT]
-    parts = [parts[0]] + [in_plane(parts[k], k) for k in range(1, SPLIT)]
+    parts = [parts[0]] + [in_plane(parts[k], k) for k in reversed(range(1, SPLIT))]
     gate_grad, up_grad, down_grad, token = pl.pallas_call(
         grads_kernel,
         out_shape=[like((half, width), BF16)] * 3 + [like((8, 128), F32)],
@@ -354,7 +357,7 @@
         [like((FOLDS * CORES * MOST, fold), BF16)] * live,
         [*parts, token],
     )
-    chunks = [chunks[0]] + [along_z(chunks[d], d) for d in range(1, live)]
+    chunks = [chunks[0]] + [along_z(chunks[d], d) for d in reversed(range(1, live))]
     back, over = call(
         lambda *refs: split_kernel(live, *refs),
         "split_rows",

time: 56.8 us -> 58 us (1.021)
  waiting for transfers between devices: 21 us -> 21.9 us
    ppermute x9, waiting for transfers between devices: 8.16 us -> 10.7 us  [in_plane(): return lax.ppermute(array, ('expert', 'dp'), hop)]
    ppermute x6, waiting for transfers between devices: 8.64 us -> 6.95 us  [along_z(): return lax.ppermute(array, 'expert', hop)]
    ppermute x6, starting transfers between devices: 10 us -> 11 us  [along_z(): return lax.ppermute(array, 'expert', hop)]
    ppermute x9, starting transfers between devices: 12 us -> 11.3 us  [in_plane(): return lax.ppermute(array, ('expert', 'dp'), hop)]
where the time goes in v3:
time: 58 us; the launch traced here: 57.8 us
  starting transfers between devices  23 us (40%)
  waiting for transfers between devices  21.9 us (38%)
  Pallas kernels  11.2 us (19%)
  local copies, waits for them, and re-layouts  0.93 us (2%)
  between operations  0.8 us (1%)
    ppermute x9, starting transfers between devices, in_plane(): return lax.ppermute(array, ('expert', 'dp'), hop)  11.3 us
    ppermute x6, starting transfers between devices, along_z(): return lax.ppermute(array, 'expert', hop)  11 us
    ppermute x9, waiting for transfers between devices, in_plane(): return lax.ppermute(array, ('expert', 'dp'), hop)  10.7 us
    ppermute x6, waiting for transfers between devices, along_z(): return lax.ppermute(array, 'expert', hop)  6.95 us
    pallas_call x9, Pallas kernels, call(): pl.pallas_call(kernel, out_shape=out_shape, in_specs=[vmem] * len(operand...  6.12 us
    ppermute x4, waiting for transfers between devices, swap_cores(): return lax.ppermute(array, 'dp', [(r, r ^ 1) for r in range(CORES)])  4.19 us
    pallas_call x1, Pallas kernels, body(): pl.pallas_call(lambda *refs: gather_kernel(live, *refs), out_shape=[gathe...  2.6 us
    pallas_call x1, Pallas kernels, body(): pl.pallas_call(grads_kernel, out_shape=[like((half, width), BF16)] * 3 +...  2.51 us
  transfers between devices with their start and end apart: 19, of which 13 were waited for; matrix products, arithmetic and copies ran while one was open for 0% of the time, Pallas kernels for 9%

profile of v3, /device:TPU:0, one launch (start us, length us, event | category | flops | bytes accessed | tf_op | source)
XLA Modules:
  0.0 57.8 jit_solution(6858070957783544174)
XLA Ops:
  0.6 2.6 %gather_rows.1 = (bf16[40,1792]{1,0:T(8,128)(2,1)}, bf16[40,1792]{1,0:T(8,128)(2,1)}, f32[32,128]{1,0:T(8,128)}) custom-call(s32[8,128]{1,0:T(8,128)} %bitcast.3, s32[8,128]{1,0:T(8,128)} %bitcast.4, f32[8,128]{1,0:T(8,128)} %bitcast.5, bf16[128,3584]{1,0:T(8,128)(2,1)} %refs_3_.1, bf16[128,3584]{1,0:T(8,128)(2,1)} %refs_4_.4), custom_call_target="tpu_custom_call" | custom-call | tf_op jit(solution)/shard_map/gather_rows/pallas_call | solution.py:281
  3.2 0.5 collective-permute-start
  3.8 1.2 %collective-permute-done.refs_1_ = bf16[40,1792]{1,0:T(8,128)(2,1)S(1)} collective-permute-done((bf16[40,1792]{1,0:T(8,128)(2,1)}, bf16[40,1792]{1,0:T(8,128)(2,1)S(1)}, u32[]{:S(2)}, u32[]{:S(2)}) %collective-permute-start) | collective-permute-done | bytes 143392 | tf_op jit(solution)/shard_map/ppermute | solution.py:267
  5.0 0.0 copy-start.4
  5.0 0.9 %copy-done.4 = bf16[40,1792]{1,0:T(8,128)(2,1)S(1)} copy-done((bf16[40,1792]{1,0:T(8,128)(2,1)S(1)}, bf16[40,1792]{1,0:T(8,128)(2,1)}, u32[]{:S(2)}) %copy-start.4) | copy-done | bytes 143384
  5.9 0.4 chunk_rows.1
  6.3 3.0 %collective-permute-start.3 = (bf16[40,896]{1,0:T(8,128)(2,1)S(1)}, bf16[40,896]{1,0:T(8,128)(2,1)S(1)}, u32[]{:S(2)}, u32[]{:S(2)}) collective-permute-start(bf16[40,896]{1,0:T(8,128)(2,1)S(1)} %get-tuple-element.39), channel_id=1, source_target_pairs={{0,8},{2,10},{4,12},{6,14},{8,0},{10,2},{12,4},{14,6},{16,24},{18,... | collective-permute-start | bytes 215048 | tf_op jit(solution)/shard_map/ppermute | solution.py:271
  9.3 2.6 %collective-permute-start.1 = (bf16[40,896]{1,0:T(8,128)(2,1)S(1)}, bf16[40,896]{1,0:T(8,128)(2,1)S(1)}, u32[]{:S(2)}, u32[]{:S(2)}) collective-permute-start(bf16[40,896]{1,0:T(8,128)(2,1)S(1)} %get-tuple-element.36), channel_id=1, source_target_pairs={{0,16},{2,18},{4,20},{6,22},{8,24},{10,26},{12,28},{14,30},{16,0},... | collective-permute-start | bytes 215048 | tf_op jit(solution)/shard_map/ppermute | solution.py:271
  11.8 0.0 collective-permute-start.2
  11.8 0.0 collective-permute-done.3.refs_1_
  11.8 0.2 merge_rows.3.refs_0_
  12.1 0.0 copy-start
  12.1 0.0 copy-start.1
  12.1 0.0 copy-start.2
  12.1 1.8 %collective-permute-start.8 = (bf16[40,1792]{1,0:T(8,128)(2,1)S(1)}, bf16[40,1792]{1,0:T(8,128)(2,1)S(1)}, u32[]{:S(2)}, u32[]{:S(2)}) collective-permute-start(bf16[40,1792]{1,0:T(8,128)(2,1)S(1)} %merge_rows.3.refs_0_), channel_id=1, source_target_pairs={{0,2},{1,5},{2,0},{3,7},{4,6},{5,1},{6,4},{7,3},{8,10},{9,13},{10,... | collective-permute-start | bytes 430088 | tf_op jit(solution)/shard_map/ppermute | solution.py:278
  13.9 1.5 %collective-permute-start.4 = (bf16[40,1792]{1,0:T(8,128)(2,1)S(1)}, bf16[40,1792]{1,0:T(8,128)(2,1)S(1)}, u32[]{:S(2)}, u32[]{:S(2)}) collective-permute-start(bf16[40,1792]{1,0:T(8,128)(2,1)S(1)} %merge_rows.3.refs_0_), channel_id=1, source_target_pairs={{0,4},{1,3},{2,6},{3,1},{4,0},{5,7},{6,2},{7,5},{8,12},{9,11},{10,... | collective-permute-start | bytes 430088 | tf_op jit(solution)/shard_map/ppermute | solution.py:278
  15.4 1.8 %collective-permute-done.1.refs_0_ = bf16[40,896]{1,0:T(8,128)(2,1)S(1)} collective-permute-done((bf16[40,896]{1,0:T(8,128)(2,1)S(1)}, bf16[40,896]{1,0:T(8,128)(2,1)S(1)}, u32[]{:S(2)}, u32[]{:S(2)}) %collective-permute-start.1) | collective-permute-done | bytes 71712 | tf_op jit(solution)/shard_map/ppermute | solution.py:271
  17.2 0.9 %collective-permute-done.2.refs_1_ = bf16[40,896]{1,0:T(8,128)(2,1)S(1)} collective-permute-done((bf16[40,896]{1,0:T(8,128)(2,1)S(1)}, bf16[40,896]{1,0:T(8,128)(2,1)S(1)}, u32[]{:S(2)}, u32[]{:S(2)}) %collective-permute-start.2) | collective-permute-done | bytes 71712 | tf_op jit(solution)/shard_map/ppermute | solution.py:271
  18.1 0.2 merge_rows.2.refs_0_
  18.3 0.7 %collective-permute-done.4.refs_2_ = bf16[40,1792]{1,0:T(8,128)(2,1)S(1)} collective-permute-done((bf16[40,1792]{1,0:T(8,128)(2,1)S(1)}, bf16[40,1792]{1,0:T(8,128)(2,1)S(1)}, u32[]{:S(2)}, u32[]{:S(2)}) %collective-permute-start.4) | collective-permute-done | bytes 143392 | tf_op jit(solution)/shard_map/ppermute | solution.py:278
  19.0 0.9 %collective-permute-start.5 = (bf16[40,1792]{1,0:T(8,128)(2,1)S(1)}, bf16[40,1792]{1,0:T(8,128)(2,1)S(1)}, u32[]{:S(2)}, u32[]{:S(2)}) collective-permute-start(bf16[40,1792]{1,0:T(8,128)(2,1)S(1)} %merge_rows.2.refs_0_), channel_id=1, source_target_pairs={{0,2},{1,5},{2,0},{3,7},{4,6},{5,1},{6,4},{7,3},{8,10},{9,13},{10,... | collective-permute-start | bytes 430088 | tf_op jit(solution)/shard_map/ppermute | solution.py:278
  19.9 0.0 collective-permute-done.8.refs_1_
  19.9 1.5 %collective-permute-start.9 = (bf16[40,1792]{1,0:T(8,128)(2,1)S(1)}, bf16[40,1792]{1,0:T(8,128)(2,1)S(1)}, u32[]{:S(2)}, u32[]{:S(2)}) collective-permute-start(bf16[40,1792]{1,0:T(8,128)(2,1)S(1)} %collective-permute-done.8.refs_1_), channel_id=1, source_target_pairs={{0,4},{1,3},{2,6},{3,1},{4,0},{5,7},{6,2},{7,5},{8,12},{9,11},{10,... | collective-permute-start | bytes 430088 | tf_op jit(solution)/shard_map/ppermute | solution.py:278
  21.4 0.5 collective-permute-start.6
  21.9 3.8 %collective-permute-done.5.refs_1_ = bf16[40,1792]{1,0:T(8,128)(2,1)S(1)} collective-permute-done((bf16[40,1792]{1,0:T(8,128)(2,1)S(1)}, bf16[40,1792]{1,0:T(8,128)(2,1)S(1)}, u32[]{:S(2)}, u32[]{:S(2)}) %collective-permute-start.5) | collective-permute-done | bytes 143392 | tf_op jit(solution)/shard_map/ppermute | solution.py:278
  25.7 1.5 %collective-permute-start.7 = (bf16[40,1792]{1,0:T(8,128)(2,1)S(1)}, bf16[40,1792]{1,0:T(8,128)(2,1)S(1)}, u32[]{:S(2)}, u32[]{:S(2)}) collective-permute-start(bf16[40,1792]{1,0:T(8,128)(2,1)S(1)} %collective-permute-done.5.refs_1_), channel_id=1, source_target_pairs={{0,4},{1,3},{2,6},{3,1},{4,0},{5,7},{6,2},{7,5},{8,12},{9,11},{10,... | collective-permute-start | bytes 430088 | tf_op jit(solution)/shard_map/ppermute | solution.py:278
  27.1 0.0 collective-permute-done.9.refs_3_
  27.2 0.0 copy-done
  27.2 0.0 copy-done.1
  27.2 0.0 copy-done.2
  27.2 1.0 %partial_products.3 = (f32[80,1152]{1,0:T(8,128)S(1)}, bf16[80,1792]{1,0:T(8,128)(2,1)S(1)}, bf16[80,1792]{1,0:T(8,128)(2,1)S(1)}) custom-call(bf16[40,1792]{1,0:T(8,128)(2,1)S(1)} %merge_rows.3.refs_0_, bf16[40,1792]{1,0:T(8,128)(2,1)S(1)} %collective-permute-done.8.refs_1_, bf16[40,1792]{1,0:T(8,128)(2,1)S(1)} %collective-permute-done.4.refs_2_, ...), custom_call_target="tpu_custom_call" | custom-call | flops 330301440 | bytes 4128768 | tf_op jit(solution)/shard_map/partial_products/pallas_call | solution.py:256
  28.2 0.1 collective-permute-start.11
  28.3 0.0 collective-permute-done.6.refs_2_
  28.3 2.5 %collective-permute-done.7.refs_3_ = bf16[40,1792]{1,0:T(8,128)(2,1)S(1)} collective-permute-done((bf16[40,1792]{1,0:T(8,128)(2,1)S(1)}, bf16[40,1792]{1,0:T(8,128)(2,1)S(1)}, u32[]{:S(2)}, u32[]{:S(2)}) %collective-permute-start.7) | collective-permute-done | bytes 143392 | tf_op jit(solution)/shard_map/ppermute | solution.py:278
  30.8 1.0 %partial_products.2 = (f32[80,1152]{1,0:T(8,128)S(1)}, bf16[80,1792]{1,0:T(8,128)(2,1)S(1)}, bf16[80,1792]{1,0:T(8,128)(2,1)S(1)}) custom-call(bf16[40,1792]{1,0:T(8,128)(2,1)S(1)} %merge_rows.2.refs_0_, bf16[40,1792]{1,0:T(8,128)(2,1)S(1)} %collective-permute-done.5.refs_1_, bf16[40,1792]{1,0:T(8,128)(2,1)S(1)} %collective-permute-done.6.refs_2_, ...), custom_call_target="tpu_custom_call" | custom-call | flops 330301440 | bytes 4128768 | tf_op jit(solution)/shard_map/partial_products/pallas_call | solution.py:256
  31.8 0.1 collective-permute-start.10
  31.9 0.0 collective-permute-done.11.refs_3_
  31.9 1.7 %collective-permute-done.10.refs_2_ = f32[80,1152]{1,0:T(8,128)S(1)} collective-permute-done((f32[80,1152]{1,0:T(8,128)S(1)}, f32[80,1152]{1,0:T(8,128)S(1)}, u32[]{:S(2)}, u32[]{:S(2)}) %collective-permute-start.10) | collective-permute-done | bytes 368672 | tf_op jit(solution)/shard_map/ppermute | solution.py:267
  33.5 1.4 %sides_and_parts.1 = (bf16[40,1792]{1,0:T(8,128)(2,1)S(1)}, bf16[40,1792]{1,0:T(8,128)(2,1)S(1)}, bf16[40,1792]{1,0:T(8,128)(2,1)S(1)}, bf16[40,1792]{1,0:T(8,128)(2,1)S(1)}, bf16[160,1152]{1,0:T(8,128)(2,1)S(1)}) custom-call(f32[80,1152]{1,0:T(8,128)S(1)} %get-tuple-element.41.refs_0_, f32[80,1152]{1,0:T(8,128)S(1)} %get-tuple-element.42.refs_1_, ...), custom_call_target="tpu_custom_call" | custom-call | flops 440401920 | bytes 2752512 | tf_op jit(solution)/shard_map/sides_and_parts/pallas_call | solution.py:256
  35.0 1.8 %collective-permute-start.12 = (bf16[40,1792]{1,0:T(8,128)(2,1)S(1)}, bf16[40,1792]{1,0:T(8,128)(2,1)S(1)}, u32[]{:S(2)}, u32[]{:S(2)}) collective-permute-start(bf16[40,1792]{1,0:T(8,128)(2,1)S(1)} %get-tuple-element.44), channel_id=1, source_target_pairs={{0,6},{1,7},{2,4},{3,5},{4,2},{5,3},{6,0},{7,1},{8,14},{9,15},{10,... | collective-permute-start | bytes 430088 | tf_op jit(solution)/shard_map/ppermute | solution.py:278
  36.8 0.5 collective-permute-start.13
  37.3 1.2 %collective-permute-start.14 = (bf16[40,1792]{1,0:T(8,128)(2,1)S(1)}, bf16[40,1792]{1,0:T(8,128)(2,1)S(1)}, u32[]{:S(2)}, u32[]{:S(2)}) collective-permute-start(bf16[40,1792]{1,0:T(8,128)(2,1)S(1)} %get-tuple-element.46), channel_id=1, source_target_pairs={{0,2},{1,5},{2,0},{3,7},{4,6},{5,1},{6,4},{7,3},{8,10},{9,13},{10,... | collective-permute-start | bytes 430088 | tf_op jit(solution)/shard_map/ppermute | solution.py:278
  38.5 0.0 copy-start.3
  38.5 2.5 %weight_grads.1 = (bf16[1792,384]{1,0:T(8,128)(2,1)}, bf16[1792,384]{1,0:T(8,128)(2,1)}, bf16[1792,384]{1,0:T(8,128)(2,1)}, f32[8,128]{1,0:T(8,128)S(1)}) custom-call(bf16[80,1792]{1,0:T(8,128)(2,1)S(1)} %get-tuple-element.47.refs_0_, bf16[80,1792]{1,0:T(8,128)(2,1)S(1)} %get-tuple-element.48.refs_1_, bf16[80,1792]{1,0:T(8,128)(2,1)S(1)} %get-tuple-element.49.refs_2_, ...), custom_call_target="tpu_custom_call" | custom-call | flops 660602880 | bytes 5275648 | tf_op jit(solution)/shard_map/weight_grads/pallas_call | solution.py:344
  41.1 1.5 %collective-permute-done.12.refs_1_ = bf16[40,1792]{1,0:T(8,128)(2,1)S(1)} collective-permute-done((bf16[40,1792]{1,0:T(8,128)(2,1)S(1)}, bf16[40,1792]{1,0:T(8,128)(2,1)S(1)}, u32[]{:S(2)}, u32[]{:S(2)}) %collective-permute-start.12) | collective-permute-done | bytes 143392 | tf_op jit(solution)/shard_map/ppermute | solution.py:278
  42.5 2.3 %collective-permute-done.13.refs_2_ = bf16[40,1792]{1,0:T(8,128)(2,1)S(1)} collective-permute-done((bf16[40,1792]{1,0:T(8,128)(2,1)S(1)}, bf16[40,1792]{1,0:T(8,128)(2,1)S(1)}, u32[]{:S(2)}, u32[]{:S(2)}) %collective-permute-start.13) | collective-permute-done | bytes 143392 | tf_op jit(solution)/shard_map/ppermute | solution.py:278
  44.8 0.1 collective-permute-done.14.refs_3_
  44.9 0.3 sum_parts.1
  45.1 4.8 %collective-permute-start.15 = (bf16[20,896]{1,0:T(8,128)(2,1)S(1)}, bf16[20,896]{1,0:T(8,128)(2,1)S(1)}, u32[]{:S(2)}, u32[]{:S(2)}) collective-permute-start(bf16[20,896]{1,0:T(8,128)(2,1)S(1)} %get-tuple-element.54), channel_id=1, source_target_pairs={{0,24},{2,26},{4,28},{6,30},{8,16},{10,18},{12,20},{14,22},{16,8},... | collective-permute-start | bytes 107528 | tf_op jit(solution)/shard_map/ppermute | solution.py:271
  49.9 0.0 collective-permute-start.16
  49.9 0.6 %collective-permute-start.17 = (bf16[20,896]{1,0:T(8,128)(2,1)S(1)}, bf16[20,896]{1,0:T(8,128)(2,1)S(1)}, u32[]{:S(2)}, u32[]{:S(2)}) collective-permute-start(bf16[20,896]{1,0:T(8,128)(2,1)S(1)} %get-tuple-element.56), channel_id=1, source_target_pairs={{0,8},{2,10},{4,12},{6,14},{8,0},{10,2},{12,4},{14,6},{16,24},{18,... | collective-permute-start | bytes 107528 | tf_op jit(solution)/shard_map/ppermute | solution.py:271
  50.6 1.5 %collective-permute-done.15.refs_1_ = bf16[20,896]{1,0:T(8,128)(2,1)S(1)} collective-permute-done((bf16[20,896]{1,0:T(8,128)(2,1)S(1)}, bf16[20,896]{1,0:T(8,128)(2,1)S(1)}, u32[]{:S(2)}, u32[]{:S(2)}) %collective-permute-start.15) | collective-permute-done | bytes 35872 | tf_op jit(solution)/shard_map/ppermute | solution.py:271
  52.0 2.8 %collective-permute-done.16.refs_2_ = bf16[20,896]{1,0:T(8,128)(2,1)S(1)} collective-permute-done((bf16[20,896]{1,0:T(8,128)(2,1)S(1)}, bf16[20,896]{1,0:T(8,128)(2,1)S(1)}, u32[]{:S(2)}, u32[]{:S(2)}) %collective-permute-start.16) | collective-permute-done | bytes 35872 | tf_op jit(solution)/shard_map/ppermute | solution.py:271
  54.8 0.0 collective-permute-done.17.refs_3_
  54.9 0.2 split_rows.1
  55.1 0.1 collective-permute-start.18
  55.2 1.3 %collective-permute-done.18.other_ref = bf16[32,1792]{1,0:T(8,128)(2,1)S(1)} collective-permute-done((bf16[32,1792]{1,0:T(8,128)(2,1)S(1)}, bf16[32,1792]{1,0:T(8,128)(2,1)S(1)}, u32[]{:S(2)}, u32[]{:S(2)}) %collective-permute-start.18) | collective-permute-done | bytes 114720 | tf_op jit(solution)/shard_map/ppermute | solution.py:267
  56.5 0.0 copy-done.3
  56.5 1.3 %place_rows.1 = bf16[128,3584]{1,0:T(8,128)(2,1)} custom-call(f32[32,128]{1,0:T(8,128)S(1)} %copy-done.3, bf16[32,1792]{1,0:T(8,128)(2,1)S(1)} %get-tuple-element.57.mine_ref, bf16[32,1792]{1,0:T(8,128)(2,1)S(1)} %collective-permute-done.18.other_ref), custom_call_target="tpu_custom_call" | custom-call | tf_op jit(solution)/shard_map/place_rows/pallas_call | solution.py:256
Async XLA Ops:
  3.2 1.7 %collective-permute-start = (bf16[40,1792]{1,0:T(8,128)(2,1)}, bf16[40,1792]{1,0:T(8,128)(2,1)S(1)}, u32[]{:S(2)}, u32[]{:S(2)}) collective-permute-start(bf16[40,1792]{1,0:T(8,128)(2,1)} %get-tuple-element.35), channel_id=1, source_target_pairs={{0,1},{1,0},{2,3},{3,2},{4,5},{5,4},{6,7},{7,6},{8,9},{9,8},{10,11... | collective-permute-start | bytes 430088 | tf_op jit(solution)/shard_map/ppermute | solution.py:267
  5.0 0.9 %copy-start.4 = (bf16[40,1792]{1,0:T(8,128)(2,1)S(1)}, bf16[40,1792]{1,0:T(8,128)(2,1)}, u32[]{:S(2)}) copy-start(bf16[40,1792]{1,0:T(8,128)(2,1)} %get-tuple-element.34.refs_0_) | copy-start | bytes 430084
  6.3 5.6 %collective-permute-start.3 = (bf16[40,896]{1,0:T(8,128)(2,1)S(1)}, bf16[40,896]{1,0:T(8,128)(2,1)S(1)}, u32[]{:S(2)}, u32[]{:S(2)}) collective-permute-start(bf16[40,896]{1,0:T(8,128)(2,1)S(1)} %get-tuple-element.39), channel_id=1, source_target_pairs={{0,8},{2,10},{4,12},{6,14},{8,0},{10,2},{12,4},{14,6},{16,24},{18,... | collective-permute-start | bytes 215048 | tf_op jit(solution)/shard_map/ppermute | solution.py:271
  9.3 7.9 %collective-permute-start.1 = (bf16[40,896]{1,0:T(8,128)(2,1)S(1)}, bf16[40,896]{1,0:T(8,128)(2,1)S(1)}, u32[]{:S(2)}, u32[]{:S(2)}) collective-permute-start(bf16[40,896]{1,0:T(8,128)(2,1)S(1)} %get-tuple-element.36), channel_id=1, source_target_pairs={{0,16},{2,18},{4,20},{6,22},{8,24},{10,26},{12,28},{14,30},{16,0},... | collective-permute-start | bytes 215048 | tf_op jit(solution)/shard_map/ppermute | solution.py:271
  11.8 6.2 %collective-permute-start.2 = (bf16[40,896]{1,0:T(8,128)(2,1)S(1)}, bf16[40,896]{1,0:T(8,128)(2,1)S(1)}, u32[]{:S(2)}, u32[]{:S(2)}) collective-permute-start(bf16[40,896]{1,0:T(8,128)(2,1)S(1)} %get-tuple-element.37), channel_id=1, source_target_pairs={{0,24},{2,26},{4,28},{6,30},{8,16},{10,18},{12,20},{14,22},{16,8},... | collective-permute-start | bytes 215048 | tf_op jit(solution)/shard_map/ppermute | solution.py:271
  12.1 15.1 %copy-start = (bf16[1792,384]{1,0:T(8,128)(2,1)S(1)}, bf16[1792,384]{1,0:T(8,128)(2,1)}, u32[]{:S(2)}) copy-start(bf16[1792,384]{1,0:T(8,128)(2,1)} %refs_4_.7) | copy-start | bytes 4128772
  12.1 15.1 %copy-start.1 = (bf16[1792,384]{1,0:T(8,128)(2,1)S(1)}, bf16[1792,384]{1,0:T(8,128)(2,1)}, u32[]{:S(2)}) copy-start(bf16[1792,384]{1,0:T(8,128)(2,1)} %refs_5_.5) | copy-start | bytes 4128772
  12.1 15.1 %copy-start.2 = (bf16[1792,384]{1,0:T(8,128)(2,1)S(1)}, bf16[1792,384]{1,0:T(8,128)(2,1)}, u32[]{:S(2)}) copy-start(bf16[1792,384]{1,0:T(8,128)(2,1)} %refs_6_.3) | copy-start | bytes 4128772
  12.1 7.8 %collective-permute-start.8 = (bf16[40,1792]{1,0:T(8,128)(2,1)S(1)}, bf16[40,1792]{1,0:T(8,128)(2,1)S(1)}, u32[]{:S(2)}, u32[]{:S(2)}) collective-permute-start(bf16[40,1792]{1,0:T(8,128)(2,1)S(1)} %merge_rows.3.refs_0_), channel_id=1, source_target_pairs={{0,2},{1,5},{2,0},{3,7},{4,6},{5,1},{6,4},{7,3},{8,10},{9,13},{10,... | collective-permute-start | bytes 430088 | tf_op jit(solution)/shard_map/ppermute | solution.py:278
  13.9 5.1 %collective-permute-start.4 = (bf16[40,1792]{1,0:T(8,128)(2,1)S(1)}, bf16[40,1792]{1,0:T(8,128)(2,1)S(1)}, u32[]{:S(2)}, u32[]{:S(2)}) collective-permute-start(bf16[40,1792]{1,0:T(8,128)(2,1)S(1)} %merge_rows.3.refs_0_), channel_id=1, source_target_pairs={{0,4},{1,3},{2,6},{3,1},{4,0},{5,7},{6,2},{7,5},{8,12},{9,11},{10,... | collective-permute-start | bytes 430088 | tf_op jit(solution)/shard_map/ppermute | solution.py:278
  19.0 6.7 %collective-permute-start.5 = (bf16[40,1792]{1,0:T(8,128)(2,1)S(1)}, bf16[40,1792]{1,0:T(8,128)(2,1)S(1)}, u32[]{:S(2)}, u32[]{:S(2)}) collective-permute-start(bf16[40,1792]{1,0:T(8,128)(2,1)S(1)} %merge_rows.2.refs_0_), channel_id=1, source_target_pairs={{0,2},{1,5},{2,0},{3,7},{4,6},{5,1},{6,4},{7,3},{8,10},{9,13},{10,... | collective-permute-start | bytes 430088 | tf_op jit(solution)/shard_map/ppermute | solution.py:278
  19.9 7.3 %collective-permute-start.9 = (bf16[40,1792]{1,0:T(8,128)(2,1)S(1)}, bf16[40,1792]{1,0:T(8,128)(2,1)S(1)}, u32[]{:S(2)}, u32[]{:S(2)}) collective-permute-start(bf16[40,1792]{1,0:T(8,128)(2,1)S(1)} %collective-permute-done.8.refs_1_), channel_id=1, source_target_pairs={{0,4},{1,3},{2,6},{3,1},{4,0},{5,7},{6,2},{7,5},{8,12},{9,11},{10,... | collective-permute-start | bytes 430088 | tf_op jit(solution)/shard_map/ppermute | solution.py:278
  21.4 6.8 %collective-permute-start.6 = (bf16[40,1792]{1,0:T(8,128)(2,1)S(1)}, bf16[40,1792]{1,0:T(8,128)(2,1)S(1)}, u32[]{:S(2)}, u32[]{:S(2)}) collective-permute-start(bf16[40,1792]{1,0:T(8,128)(2,1)S(1)} %merge_rows.2.refs_0_), channel_id=1, source_target_pairs={{0,4},{1,3},{2,6},{3,1},{4,0},{5,7},{6,2},{7,5},{8,12},{9,11},{10,... | collective-permute-start | bytes 430088 | tf_op jit(solution)/shard_map/ppermute | solution.py:278
  25.7 5.1 %collective-permute-start.7 = (bf16[40,1792]{1,0:T(8,128)(2,1)S(1)}, bf16[40,1792]{1,0:T(8,128)(2,1)S(1)}, u32[]{:S(2)}, u32[]{:S(2)}) collective-permute-start(bf16[40,1792]{1,0:T(8,128)(2,1)S(1)} %collective-permute-done.5.refs_1_), channel_id=1, source_target_pairs={{0,4},{1,3},{2,6},{3,1},{4,0},{5,7},{6,2},{7,5},{8,12},{9,11},{10,... | collective-permute-start | bytes 430088 | tf_op jit(solution)/shard_map/ppermute | solution.py:278
  28.2 3.7 %collective-permute-start.11 = (f32[80,1152]{1,0:T(8,128)S(1)}, f32[80,1152]{1,0:T(8,128)S(1)}, u32[]{:S(2)}, u32[]{:S(2)}) collective-permute-start(f32[80,1152]{1,0:T(8,128)S(1)} %get-tuple-element.42.refs_1_), channel_id=1, source_target_pairs={{0,1},{1,0},{2,3},{3,2},{4,5},{5,4},{6,7},{7,6},{8,9},{9,8},{10,11... | collective-permute-start | bytes 1105928 | tf_op jit(solution)/shard_map/ppermute | solution.py:267
  31.8 1.8 %collective-permute-start.10 = (f32[80,1152]{1,0:T(8,128)S(1)}, f32[80,1152]{1,0:T(8,128)S(1)}, u32[]{:S(2)}, u32[]{:S(2)}) collective-permute-start(f32[80,1152]{1,0:T(8,128)S(1)} %get-tuple-element.41.refs_0_), channel_id=1, source_target_pairs={{0,1},{1,0},{2,3},{3,2},{4,5},{5,4},{6,7},{7,6},{8,9},{9,8},{10,11... | collective-permute-start | bytes 1105928 | tf_op jit(solution)/shard_map/ppermute | solution.py:267
  35.0 7.6 %collective-permute-start.12 = (bf16[40,1792]{1,0:T(8,128)(2,1)S(1)}, bf16[40,1792]{1,0:T(8,128)(2,1)S(1)}, u32[]{:S(2)}, u32[]{:S(2)}) collective-permute-start(bf16[40,1792]{1,0:T(8,128)(2,1)S(1)} %get-tuple-element.44), channel_id=1, source_target_pairs={{0,6},{1,7},{2,4},{3,5},{4,2},{5,3},{6,0},{7,1},{8,14},{9,15},{10,... | collective-permute-start | bytes 430088 | tf_op jit(solution)/shard_map/ppermute | solution.py:278
  36.8 8.0 %collective-permute-start.13 = (bf16[40,1792]{1,0:T(8,128)(2,1)S(1)}, bf16[40,1792]{1,0:T(8,128)(2,1)S(1)}, u32[]{:S(2)}, u32[]{:S(2)}) collective-permute-start(bf16[40,1792]{1,0:T(8,128)(2,1)S(1)} %get-tuple-element.45), channel_id=1, source_target_pairs={{0,4},{1,3},{2,6},{3,1},{4,0},{5,7},{6,2},{7,5},{8,12},{9,11},{10,... | collective-permute-start | bytes 430088 | tf_op jit(solution)/shard_map/ppermute | solution.py:278
  37.3 7.6 %collective-permute-start.14 = (bf16[40,1792]{1,0:T(8,128)(2,1)S(1)}, bf16[40,1792]{1,0:T(8,128)(2,1)S(1)}, u32[]{:S(2)}, u32[]{:S(2)}) collective-permute-start(bf16[40,1792]{1,0:T(8,128)(2,1)S(1)} %get-tuple-element.46), channel_id=1, source_target_pairs={{0,2},{1,5},{2,0},{3,7},{4,6},{5,1},{6,4},{7,3},{8,10},{9,13},{10,... | collective-permute-start | bytes 430088 | tf_op jit(solution)/shard_map/ppermute | solution.py:278
  38.5 18.0 %copy-start.3 = (f32[32,128]{1,0:T(8,128)S(1)}, f32[32,128]{1,0:T(8,128)}, u32[]{:S(2)}) copy-start(f32[32,128]{1,0:T(8,128)} %get-tuple-element.33.hot_ref) | copy-start | bytes 49156
  45.1 6.9 %collective-permute-start.15 = (bf16[20,896]{1,0:T(8,128)(2,1)S(1)}, bf16[20,896]{1,0:T(8,128)(2,1)S(1)}, u32[]{:S(2)}, u32[]{:S(2)}) collective-permute-start(bf16[20,896]{1,0:T(8,128)(2,1)S(1)} %get-tuple-element.54), channel_id=1, source_target_pairs={{0,24},{2,26},{4,28},{6,30},{8,16},{10,18},{12,20},{14,22},{16,8},... | collective-permute-start | bytes 107528 | tf_op jit(solution)/shard_map/ppermute | solution.py:271
  49.9 4.9 %collective-permute-start.16 = (bf16[20,896]{1,0:T(8,128)(2,1)S(1)}, bf16[20,896]{1,0:T(8,128)(2,1)S(1)}, u32[]{:S(2)}, u32[]{:S(2)}) collective-permute-start(bf16[20,896]{1,0:T(8,128)(2,1)S(1)} %get-tuple-element.55), channel_id=1, source_target_pairs={{0,16},{2,18},{4,20},{6,22},{8,24},{10,26},{12,28},{14,30},{16,0},... | collective-permute-start | bytes 107528 | tf_op jit(solution)/shard_map/ppermute | solution.py:271
  49.9 4.9 %collective-permute-start.17 = (bf16[20,896]{1,0:T(8,128)(2,1)S(1)}, bf16[20,896]{1,0:T(8,128)(2,1)S(1)}, u32[]{:S(2)}, u32[]{:S(2)}) collective-permute-start(bf16[20,896]{1,0:T(8,128)(2,1)S(1)} %get-tuple-element.56), channel_id=1, source_target_pairs={{0,8},{2,10},{4,12},{6,14},{8,0},{10,2},{12,4},{14,6},{16,24},{18,... | collective-permute-start | bytes 107528 | tf_op jit(solution)/shard_map/ppermute | solution.py:271
  55.1 1.4 %collective-permute-start.18 = (bf16[32,1792]{1,0:T(8,128)(2,1)S(1)}, bf16[32,1792]{1,0:T(8,128)(2,1)S(1)}, u32[]{:S(2)}, u32[]{:S(2)}) collective-permute-start(bf16[32,1792]{1,0:T(8,128)(2,1)S(1)} %get-tuple-element.58), channel_id=1, source_target_pairs={{0,1},{1,0},{2,3},{3,2},{4,5},{5,4},{6,7},{7,6},{8,9},{9,8},{10,11... | collective-permute-start | bytes 344072 | tf_op jit(solution)/shard_map/ppermute | solution.py:267
